TPU v7x, 128 devices: a whole 4x4x4 slice. The times are simulated.
128 devices in a mesh: net: 4 (over x), line: 32 (over z, y, core).
Axes of the slice: x: 4, y: 4, z: 4, core: 2. Of those that a mesh axis runs over, the one named last changes fastest.
Arguments:
- conductance_inverse: float32 [4, 4096, 4096], P('net', 'line'), may hold values from -0.5 to 4.5, as said below
- prior_voltage: float32 [4, 96, 4096], P('net', None, 'line'), may hold values from -6 to 6
- sources: float32 [3, 4, 4096], P(None, 'net', 'line'), may hold values from -6 to 6
- fault_node: int32 [96], replicated, may hold values from 0 to 16383
- fault_conductance: float32 [96], replicated, may hold values from 0.5 to 4
- terminal_node: int32 [4, 3, 16384], P('net', None, 'line'), may hold values from 0 to 4095
- ownership: int32 [4, 16384], P('net', 'line'), may hold values from 0 to 1, as said below
- partner: int32 [4, 16384], P('net', 'line'), may hold values from 0 to 127, as said below
- delay_steps: int32 [4, 16384], P('net', 'line'), may hold values from 1 to 4, as said below
- surge_conductance: float32 [4, 16384], P('net', 'line'), may hold values from 0.2 to 1
- pole_wave: float32 [4, 6, 16384], P('net', None, 'line'), may hold values from 0.2 to 0.95
- residue_wave: float32 [4, 6, 3, 3, 16384], P('net', None, None, None, 'line'), may hold values from -1 to 1
- pole_admit: float32 [4, 6, 16384], P('net', None, 'line'), may hold values from 0.2 to 0.95
- residue_admit: float32 [4, 6, 3, 3, 16384], P('net', None, None, None, 'line'), may hold values from -1 to 1
- wave_state: float32 [4, 6, 3, 96, 16384], P('net', None, None, None, 'line'), may hold values from -4 to 4
- admit_state: float32 [4, 6, 3, 96, 16384], P('net', None, None, None, 'line'), may hold values from -4 to 4
- wave_history: float32 [4, 4, 3, 96, 16384], P('net', None, None, None, 'line'), may hold values from -6 to 6
Outputs:
- final_voltage: float32 [4, 96, 4096], P('net', None, 'line')
- end_current: float32 [4, 3, 96, 16384], P('net', None, None, 'line')
Inputs may be any that keep to these rules, and one draw needn't show every extreme that they name: `conductance_inverse`: each block is exactly symmetric. `ownership`: A slot is live exactly when the slot of the same number j % 512 at its partner owner is live; the number of live slots differs from owner to owner. The far end of slot j lies in the slot of the same number j % 512 at the partner owner, the partner of that slot is the first owner again, never the owner itself, and at most 5 live slots of one owner have the same partner; this many occur. `delay_steps`: equal at both ends of a line.
All inputs are finite; a program needn't handle non-finite values.
Results may differ from a plain program's by a relative error of at most 0.0003.
Values sent between devices are 32-bit elements; how exact they have to be, the bound alone decides.
No kernel may reach another device: no remote copies, remote signals or barrier semaphores. Data moves between devices by JAX's collectives and lax.ppermute only.
A program may use at most 128 MiB of HBM per device.

v0:
```python
import functools

import jax
import jax.numpy as jnp
from jax import lax
from jax.experimental import pallas as pl
from jax.experimental.pallas import tpu as pltpu
from jax.sharding import Mesh
from jax.sharding import PartitionSpec as P

STEPS = 3
PLANE = ("z", "y")
LINE = ("z", "y", "core")
NET_LINE = ("net", "z", "y", "core")
SIDE = 4
CHIPS = SIDE * SIDE
CAPACITY = 5
F32 = jnp.float32
BF16 = jnp.bfloat16
VMEM = pl.BlockSpec(memory_space=pltpu.VMEM)
SMEM = pl.BlockSpec(memory_space=pltpu.SMEM)
PARAMS = pltpu.CompilerParams(vmem_limit_bytes=16 * 1024 * 1024)


def shape(*dims, dtype=F32):
    return jax.ShapeDtypeStruct(dims, dtype)


def estimate(arrays, outs, flops):
    moved = sum(a.size * a.dtype.itemsize for a in [*arrays, *jax.tree.leaves(outs)])
    return pl.CostEstimate(flops=flops, bytes_accessed=moved, transcendentals=0)


def call(kernel, scalars, arrays, outs, scratch=(), flops=1_000_000):
    return pl.pallas_call(
        kernel,
        out_shape=outs,
        in_specs=[SMEM] * len(scalars) + [VMEM] * len(arrays),
        out_specs=jax.tree.map(lambda _: VMEM, outs),
        scratch_shapes=list(scratch),
        compiler_params=PARAMS,
        cost_estimate=estimate(arrays, outs, flops),
    )(*scalars, *arrays)


def halves(x):
    high = x.astype(BF16)
    low = (x - high.astype(F32)).astype(BF16)
    return high, low


def stacked(x):
    return jnp.concatenate(halves(x), axis=0)


def ones_where(mask):
    return jnp.where(mask, 1.0, 0.0).astype(BF16)


def within_block(nodes, block):
    return jnp.clip(nodes - block * 128, -1, 128).astype(F32).astype(BF16)


def hot_block(local, nodes, block):
    one, zero = jnp.ones((), BF16), jnp.zeros((), BF16)
    return jnp.where(local == within_block(nodes, block), one, zero)


def block_places(width):
    return lax.broadcasted_iota(jnp.int32, (128, width), 0).astype(F32).astype(BF16)


def dot(a, b, dims):
    return lax.dot_general(a, b, (dims, ((), ())), preferred_element_type=F32)


NN = ((1,), (0,))
NT = ((1,), (1,))
TN = ((0,), (0,))


def mix(coef, waves):
    return [
        coef[p, 0:1, :] * waves[0] + coef[p, 1:2, :] * waves[1] + coef[p, 2:3, :] * waves[2]
        for p in range(3)
    ]


def lag_coefficients(own, delay, pw, rw, pa, ra, coef):
    live = own[...]
    steps = delay[...]
    first = (steps == 1).astype(F32)
    second = (steps == 2).astype(F32)
    for p in range(3):
        lags = []
        for pole, res in ((pa, ra), (pw, rw)):
            terms = [res[q, p] for q in range(pole.shape[0])]
            for m in range(STEPS):
                if m:
                    terms = [x * pole[q : q + 1, :] for q, x in enumerate(terms)]
                lags.append(sum(terms[1:], terms[0]) * live)
        for m in range(STEPS):
            coef[m, p] = lags[m]
            coef[STEPS + 2 + m, p] = lags[STEPS + m]
        coef[STEPS, p] = lags[STEPS] * first
        coef[STEPS + 1, p] = lags[STEPS + 1] * first + lags[STEPS] * second


def fold_states(times, own, delay, pw, pa, coef, xw, xa, hist, outs):
    live = own[...]
    steps = delay[...]
    delayed = []
    for age in range(max(times) + 1):
        rows = []
        for r in range(3):
            w = None
            for k in range(hist.shape[0] - age):
                part = jnp.where(steps == k + 1 + age, hist[k, r], 0.0)
                w = part if w is None else w + part
            rows.append(w)
        delayed.append(rows)
    for p in range(3):
        totals = {}
        for q in range(pw.shape[0]):
            w_now = xw[q, p]
            a_now = xa[q, p]
            for t in range(max(times) + 1):
                w_now = w_now * pw[q : q + 1, :]
                a_now = a_now * pa[q : q + 1, :]
                if t in times:
                    part = w_now - a_now
                    totals[t] = totals[t] + part if t in totals else part
        for t, out in zip(times, outs):
            value = totals[t] * live
            for s in range(t + 1):
                lag = STEPS + 2 + t - s
                for r in range(3):
                    value = value + coef[lag, p, r : r + 1, :] * delayed[s][r]
            out[p] = value


def fold_first(own, delay, pw, rw, pa, ra, xw, xa, hist, out, coef):
    @pl.when(pl.program_id(0) == 0)
    def _():
        lag_coefficients(own, delay, pw, rw, pa, ra, coef)

    fold_states((0,), own, delay, pw, pa, coef, xw, xa, hist, (out,))


def fold_later(own, delay, pw, pa, coef, xw, xa, hist, *outs):
    fold_states((1, 2), own, delay, pw, pa, coef, xw, xa, hist, outs)


def fold(kernel, small, states, bases, coefs):
    poles, _, scenarios, slots = states[0].shape
    tile = 16
    whole = lambda a: pl.BlockSpec(a.shape, lambda i: (0,) * len(a.shape))
    cut = lambda a: pl.BlockSpec((*a.shape[:2], tile, slots), lambda i: (0, 0, i, 0))
    out = shape(3, scenarios, slots)
    outs = [out] * bases + coefs
    return pl.pallas_call(
        kernel,
        grid=(scenarios // tile,),
        out_shape=outs,
        in_specs=[whole(a) for a in small] + [cut(a) for a in states],
        out_specs=[pl.BlockSpec((3, tile, slots), lambda i: (0, i, 0))] * bases
        + [whole(a) for a in coefs],
        compiler_params=PARAMS,
        cost_estimate=estimate((*small, *states), outs, 20_000_000),
    )(*small, *states)


def cut_kernel(pos, inverse, mine, give):
    rows = inverse.shape[0]
    for k in range(CHIPS):
        lanes = slice(k * 128, (k + 1) * 128)
        start = pl.multiple_of((k * 2 + pos[0]) * 128, 128)
        high, low = halves(inverse[:, pl.ds(start, 128)])
        mine[0:rows, lanes] = high
        mine[rows : 2 * rows, lanes] = low
        start = pl.multiple_of((k * 2 + 1 - pos[0]) * 128, 128)
        give[:, lanes] = inverse[:, pl.ds(start, 128)]


def split_kernel(inverse, out):
    rows = inverse.shape[0]
    high, low = halves(inverse[...])
    out[0:rows] = high
    out[rows : 2 * rows] = low


def gather_into(side, terminal, volts, split, emit):
    count, scenarios, lanes = volts.shape
    for k in range(count):
        high, low = halves(volts[k])
        split[0:scenarios, k * lanes : (k + 1) * lanes] = high
        split[scenarios : 2 * scenarios, k * lanes : (k + 1) * lanes] = low
    width = 256
    local = block_places(width)
    for p in range(3):
        for n in range(terminal.shape[1] // width):
            cut = slice(n * width, (n + 1) * width)
            nodes = terminal[p : p + 1, cut]
            hot = jnp.concatenate(
                [hot_block(local, nodes, 2 * k + side) for k in range(count)], axis=0
            )
            both = dot(split[...], hot, NN)
            emit(p, cut, both[:scenarios] + both[scenarios:])


def gather_kernel(pos, terminal, volts, out, split):
    def emit(p, cut, value):
        out[p, :, cut] = value

    gather_into(pos[0], terminal, volts, split, emit)


def gather_rest(pos, terminal, volts, before, out, split):
    def emit(p, cut, value):
        out[p, :, cut] = before[p, :, cut] + value

    gather_into(1 - pos[0], terminal, volts, split, emit)


def scatter_into(side, terminal, split, emit):
    ends = split.shape[1]
    scenarios = split.shape[0] // 2
    local = block_places(ends)
    nodes = jnp.concatenate([terminal[p : p + 1, :] for p in range(3)], axis=1)
    for k in range(0, CHIPS, 2):
        hot = jnp.concatenate(
            [hot_block(local, nodes, 2 * (k + i) + side) for i in range(2)], axis=0
        )
        both = dot(split, hot, NT)
        value = both[:scenarios] + both[scenarios:]
        for i in range(2):
            emit(k + i, value[:, i * 128 : (i + 1) * 128])


def split_ends(h):
    parts = [stacked(h[p]) for p in range(3)]
    return jnp.concatenate(parts, axis=1)


def scatter_other(pos, terminal, h, out, split):
    def emit(k, value):
        out[k] = value

    split[...] = split_ends(h)
    scatter_into(1 - pos[0], terminal, split[...], emit)


def first_kernel(pos, terminal, volts, before, base, coef, term, h_out, out, split, ends):
    gather_rest(pos, terminal, volts, before, term, split)
    drop = mix(coef[0], term)
    for p in range(3):
        h_out[p] = base[p] - drop[p]
    scatter_other(pos, terminal, h_out, out, ends)


def scatter_mine(step, pos, terminal, h, source, drain, volts, out, split):
    def emit(k, value):
        out[k] = value

    split[...] = split_ends(h)
    scatter_into(pos[0], terminal, split[...], emit)
    me = pos[1]
    out[me] = out[me] + source[step] - drain[...] * volts[...]


def hot_places(places, count):
    owner = lax.broadcasted_iota(jnp.int32, (count, places.shape[1]), 0)
    return [ones_where(owner * 8 + r == places) for r in range(CAPACITY)]


def packed_lines(values):
    return -(-CAPACITY * values // 128)


def pack_kernel(pos, terminal, places, volts, before, surge2, h, term, packed, split):
    gather_rest(pos, terminal, volts, before, term, split)
    waves = [surge2[...] * term[p] - h[p] for p in range(3)]
    high, low = halves(jnp.concatenate(waves, axis=0))
    lines = packed_lines(high.shape[0])
    owners = packed.shape[0] // lines
    rows = []
    for hot in hot_places(places[...], owners):
        rows.append(dot(hot, high, NT) + dot(hot, low, NT))
    used = sum(r.shape[1] for r in rows)
    rows.append(jnp.zeros((owners, lines * 128 - used), F32))
    rows = jnp.concatenate(rows, axis=1)
    for k in range(lines):
        packed[pl.ds(k, owners, stride=lines), :] = rows[:, k * 128 : (k + 1) * 128]


def known_1(base, coef, t0, t1, out):
    a, b = mix(coef[1], t0), mix(coef[0], t1)
    for p in range(3):
        out[p] = base[p] - a[p] - b[p]


def known_2(base, coef, t0, t1, t2, a1, out):
    a, b, c = mix(coef[2], t0), mix(coef[1], t1), mix(coef[0], t2)
    d = mix(coef[STEPS + 1], a1)
    for p in range(3):
        out[p] = base[p] - a[p] - b[p] - c[p] + d[p]


def arrive_kernel(pos, terminal, places, packed, base, coef, arrived, h_out, out, ends):
    scenarios = base.shape[1]
    wide = 3 * scenarios
    lines = packed_lines(wide)
    owners = packed.shape[0] // lines
    rows = jnp.concatenate(
        [packed[pl.ds(k, owners, stride=lines), :] for k in range(lines)], axis=1
    )
    total = None
    for r, hot in enumerate(hot_places(places[...], owners)):
        high, low = halves(rows[:, r * wide : (r + 1) * wide])
        part = dot(high, hot, TN) + dot(low, hot, TN)
        total = part if total is None else total + part
    for p in range(3):
        arrived[p] = total[p * scenarios : (p + 1) * scenarios]
    gain = mix(coef[STEPS], arrived)
    for p in range(3):
        h_out[p] = base[p] + gain[p]
    scatter_other(pos, terminal, h_out, out, ends)


def last_kernel(pos, terminal, volts, before, surge, h, out, split):
    def emit(p, cut, value):
        term = before[p, :, cut] + value
        out[p, :, cut] = surge[:, cut] * term - h[p, :, cut]

    gather_into(1 - pos[0], terminal, volts, split, emit)


def total_kernel(parts, out):
    total = parts[0]
    for k in range(1, CHIPS):
        total = total + parts[k]
    for k in range(CHIPS):
        out[k] = total


def copies_kernel(a, b, rows, out):
    volts = a[...] + b[...]
    rows[...] = volts
    for k in range(CHIPS):
        out[k] = volts


def solve_kernel(current, inverse, out, split):
    count, scenarios, lanes = current.shape
    for k in range(count):
        high, low = halves(current[k])
        split[0:scenarios, k * lanes : (k + 1) * lanes] = high
        split[scenarios : 2 * scenarios, k * lanes : (k + 1) * lanes] = low
    both = dot(split[...], inverse[...], NT)
    out[...] = both[:scenarios, :lanes] + both[:scenarios, lanes:] + both[scenarios:, :lanes]


def exchanged(x):
    return lax.all_to_all(x, PLANE, 0, 0, tiled=True)


def swapped(x):
    return lax.ppermute(x, "core", [(0, 1), (1, 0)])


def on_device(
    conductance_inverse,
    prior_voltage,
    sources,
    fault_node,
    fault_conductance,
    terminal_node,
    ownership,
    partner,
    delay_steps,
    surge_conductance,
    pole_wave,
    residue_wave,
    pole_admit,
    residue_admit,
    wave_state,
    admit_state,
    wave_history,
):
    rows, node_count = conductance_inverse.shape[1:]
    scenarios = prior_voltage.shape[1]
    slots = ownership.shape[1]
    ends = 3 * slots
    devices = lax.axis_size(NET_LINE)
    net, z, y, core = (lax.axis_index(a) for a in NET_LINE)
    me = lax.axis_index(LINE)

    live = ownership[0] > 0
    live_float = live.astype(F32)[None]
    partners = partner[0]
    slot = jnp.arange(slots, dtype=jnp.int32)
    earlier = (
        (partners[:, None] == partners[None, :])
        & live[:, None]
        & (slot[:, None] < slot[None, :])
    )
    rank = jnp.sum(earlier.astype(jnp.int32), axis=0)
    places = jnp.where(live, partners * 8 + rank, -1)[None]
    terminal = terminal_node[0]
    surge = surge_conductance * live_float
    surge2 = 2.0 * surge
    lane = jnp.arange(rows, dtype=jnp.int32)[None]
    first_node = net * node_count + me * rows
    drain = jnp.where(
        fault_node[:, None] - first_node == lane, fault_conductance[:, None], 0.0
    )
    pos = jnp.stack([core, z * SIDE + y]).astype(jnp.int32)

    half = shape(CHIPS, scenarios, rows)
    waves = shape(3, scenarios, slots)
    splits = pltpu.VMEM((2 * scenarios, 16 * rows), BF16)
    end_split = pltpu.VMEM((2 * scenarios, ends), BF16)

    block = shape(scenarios, rows)

    def first_gather(plane):
        return call(gather_kernel, (pos,), (terminal, plane), waves, [splits], 4_000_000_000)

    def solve(h, other, step, voltage_rows):
        sent = swapped(other)
        mine = call(
            functools.partial(scatter_mine, step),
            (pos,),
            (terminal, h, sources, drain, voltage_rows),
            half,
            [end_split],
            4_000_000_000,
        )
        plane = exchanged(call(total_kernel, (), (exchanged(mine + sent),), half))
        other = call(solve_kernel, (), (plane, inverse_other), block, [splits], 500_000_000)
        sent = swapped(other)
        mine = call(solve_kernel, (), (plane, inverse_mine), block, [splits], 500_000_000)
        return call(copies_kernel, (), (mine, sent), (block, half))

    voltage_rows = prior_voltage[0]
    plane = exchanged(jnp.broadcast_to(voltage_rows[None], half.shape))
    small = (live_float, delay_steps, pole_wave[0], pole_admit[0])
    states = (wave_state[0], admit_state[0], wave_history[0])
    live_row, delays, poles_w, poles_a = small
    base_0, coef = fold(
        fold_first,
        (live_row, delays, poles_w, residue_wave[0], poles_a, residue_admit[0]),
        states,
        1,
        [shape(2 * STEPS + 2, 3, 3, slots)],
    )
    plane, base_0, coef = lax.optimization_barrier((plane, base_0, coef))
    base = [base_0, *fold(fold_later, (*small, coef), states, STEPS - 1, [])]
    inverse_mine, give = call(
        cut_kernel,
        (pos,),
        (conductance_inverse[0],),
        (shape(2 * rows, CHIPS * 128, dtype=BF16), shape(rows, CHIPS * 128)),
    )
    inverse_other = call(
        split_kernel, (), (swapped(give),), shape(2 * rows, CHIPS * 128, dtype=BF16)
    )
    far = swapped(plane)
    before = first_gather(plane)
    t0, h, other = call(
        first_kernel,
        (pos,),
        (terminal, far, before, base[0], coef),
        (waves, waves, half),
        [splits, end_split],
        8_000_000_000,
    )
    voltage_rows, copies = solve(h, other, 0, voltage_rows)
    terms = [t0]
    arrivals = []
    lines = packed_lines(3 * scenarios)
    packed_shape = shape(devices * lines, 128)
    for step in range(1, STEPS):
        plane = exchanged(copies)
        far = swapped(plane)
        before = first_gather(plane)
        term, packed = call(
            pack_kernel,
            (pos,),
            (terminal, places, far, before, surge2, h),
            (waves, packed_shape),
            [splits],
            5_000_000_000,
        )
        terms.append(term)
        packed = packed.reshape(devices, 1, lines * 128)
        packed = lax.all_to_all(packed, NET_LINE, 0, 0, tiled=True)
        packed = packed.reshape(devices * lines, 128)
        known = call((known_1, known_2)[step - 1], (), (base[step], coef, *terms, *arrivals), waves)
        arrived, h, other = call(
            arrive_kernel,
            (pos,),
            (terminal, places, packed, known, coef),
            (waves, waves, half),
            [end_split],
            5_000_000_000,
        )
        arrivals.append(arrived)
        voltage_rows, copies = solve(h, other, step, voltage_rows)
    plane = exchanged(copies)
    far = swapped(plane)
    before = first_gather(plane)
    current = call(
        last_kernel, (pos,), (terminal, far, before, surge, h), waves, [splits], 4_000_000_000
    )
    return voltage_rows[None], current[None]


def solution(mesh):
    finer = Mesh(mesh.devices.reshape(mesh.shape["net"], SIDE, SIDE, 2), NET_LINE)
    in_specs = (
        P("net", LINE, None),
        P("net", None, LINE),
        P(None, "net", LINE),
        P(),
        P(),
        P("net", None, LINE),
        P("net", LINE),
        P("net", LINE),
        P("net", LINE),
        P("net", LINE),
        P("net", None, LINE),
        P("net", None, None, None, LINE),
        P("net", None, LINE),
        P("net", None, None, None, LINE),
        P("net", None, None, None, LINE),
        P("net", None, None, None, LINE),
        P("net", None, None, None, LINE),
    )
    out_specs = (P("net", None, LINE), P("net", None, None, LINE))
    return jax.shard_map(
        on_device, mesh=finer, in_specs=in_specs, out_specs=out_specs, check_vma=False
    )
```

profile of v0, /device:TPU:1, one launch (start us, length us, event | category | flops | bytes accessed | tf_op | source)
XLA Modules:
  0.0 292.4 jit_solution(18329210386602940542)
XLA Ops:
  0.6 1.9 broadcast_in_dim.39
  2.6 8.6 %all-to-all-start = ((f32[16,96,128]{2,1,0:T(8,128)}), f32[16,96,128]{2,1,0:T(8,128)S(1)}, u32[]{:S(2)}, u32[]{:S(2)}) async-start(f32[16,96,128]{2,1,0:T(8,128)} %broadcast_in_dim.39), calls=%async_computation | async-start | bytes 1572864 | tf_op jit(solution)/shard_map/all_to_all | solution.py:364
  14.2 2.0 copy-done
  16.2 2.0 copy-done.2
  18.9 1.9 shard_map.176
  21.7 2.7 all-to-all-done.volts
  24.3 2.3 collective-permute-start
  26.7 1.9 shard_map.177.before
  28.7 4.2 %shard_map.178 = (f32[3,96,512]{2,1,0:T(8,128)S(1)}, f32[3,96,512]{2,1,0:T(8,128)S(1)}, f32[16,96,128]{2,1,0:T(8,128)S(1)}) custom-call(s32[2]{0:T(128)S(1)} %pad_add_fusion.pos, s32[3,512]{1,0:T(4,128)S(1)} %bitcast.38, f32[16,96,128]{2,1,0:T(8,128)S(1)} %collective-permute-done.volts, f32[3,96,512]{2,1,0:T(8,128)S(1)} %shard_map.177.before, ...), custom_call_target="tpu_custom_call" | custom-call | flops 8000000000 | bytes 4085760 | tf_op jit(solution)/shard_map/pallas_call | solution.py:35
  33.3 2.8 shard_map.179
  37.1 3.6 %all-to-all-start.1 = ((f32[16,96,128]{2,1,0:T(8,128)}), f32[16,96,128]{2,1,0:T(8,128)S(1)}, u32[]{:S(2)}, u32[]{:S(2)}) async-start(f32[16,96,128]{2,1,0:T(8,128)} %add.30), calls=%async_computation.1 | async-start | bytes 1572864 | tf_op jit(solution)/shard_map/all_to_all | solution.py:364
  40.8 1.6 copy-done.7
  42.4 1.8 shard_map.181
  44.5 10.0 %all-to-all-done.1.parts = f32[16,96,128]{2,1,0:T(8,128)S(1)} async-done(((f32[16,96,128]{2,1,0:T(8,128)}), f32[16,96,128]{2,1,0:T(8,128)S(1)}, u32[]{:S(2)}, u32[]{:S(2)}) %all-to-all-start.1) | async-done | bytes 786464 | tf_op jit(solution)/shard_map/all_to_all | solution.py:364
  55.5 3.7 %all-to-all-start.2 = ((f32[16,96,128]{2,1,0:T(8,128)}), f32[16,96,128]{2,1,0:T(8,128)S(1)}, u32[]{:S(2)}, u32[]{:S(2)}) async-start(f32[16,96,128]{2,1,0:T(8,128)} %copy-done.6), calls=%async_computation.2 | async-start | bytes 1572864 | tf_op jit(solution)/shard_map/all_to_all | solution.py:364
  60.6 11.4 %all-to-all-done.2.current = f32[16,96,128]{2,1,0:T(8,128)S(1)} async-done(((f32[16,96,128]{2,1,0:T(8,128)}), f32[16,96,128]{2,1,0:T(8,128)S(1)}, u32[]{:S(2)}, u32[]{:S(2)}) %all-to-all-start.2) | async-done | bytes 786464 | tf_op jit(solution)/shard_map/all_to_all | solution.py:364
  72.5 2.6 collective-permute-start.3
  77.6 3.6 %all-to-all-start.3 = ((f32[16,96,128]{2,1,0:T(8,128)}), f32[16,96,128]{2,1,0:T(8,128)S(1)}, u32[]{:S(2)}, u32[]{:S(2)}) async-start(f32[16,96,128]{2,1,0:T(8,128)} %copy-done.12), calls=%async_computation.3 | async-start | bytes 1572864 | tf_op jit(solution)/shard_map/all_to_all | solution.py:364
  81.2 1.6 convert_reduce_fusion
  82.8 12.2 %all-to-all-done.3.volts = f32[16,96,128]{2,1,0:T(8,128)S(1)} async-done(((f32[16,96,128]{2,1,0:T(8,128)}), f32[16,96,128]{2,1,0:T(8,128)S(1)}, u32[]{:S(2)}, u32[]{:S(2)}) %all-to-all-start.3) | async-done | bytes 786464 | tf_op jit(solution)/shard_map/all_to_all | solution.py:364
  95.0 1.5 collective-permute-start.4
  99.8 2.0 shard_map.186.before
  101.8 3.2 %shard_map.187 = (f32[3,96,512]{2,1,0:T(8,128)S(1)}, f32[1536,128]{1,0:T(8,128)S(1)}) custom-call(s32[2]{0:T(128)S(1)} %copy-done.41, s32[3,512]{1,0:T(4,128)S(1)} %bitcast.41, s32[1,512]{1,0:T(1,128)S(1)} %add_select_fusion.places, f32[16,96,128]{2,1,0:T(8,128)S(1)} %collective-permute-done.4.volts, f32[3,96,512]{2,1,0:T(8,128)S(1)} %shard_map.186.before, ...), custom_call_target="tpu_custom_call" | custom-call | flops 5000000000 | bytes 3352576 | tf_op jit(solution)/shard_map/pallas_call | solution.py:35
  105.9 5.7 %all-to-all-start.4 = ((f32[128,1,1536]{2,1,0:T(1,128)}), f32[128,1,1536]{2,1,0:T(1,128)}, u32[]{:S(2)}, u32[]{:S(2)}) async-start(f32[128,1,1536]{2,1,0:T(1,128)} %bitcast.33), calls=%async_computation.4 | async-start | bytes 1572864 | tf_op jit(solution)/shard_map/all_to_all | solution.py:497
  111.6 2.0 copy-done.1
  113.6 2.0 copy-done.3
  115.6 1.7 copy-done.5
  118.6 3.2 %shard_map.188 = (f32[3,96,512]{2,1,0:T(8,128)S(1)}, f32[3,96,512]{2,1,0:T(8,128)S(1)}) custom-call(f32[1,512]{1,0:T(1,128)S(1)} %copy-done.25, s32[1,512]{1,0:T(1,128)S(1)} %copy-done.27, f32[6,512]{1,0:T(8,128)S(1)} %get-tuple-element.63.pw, f32[6,512]{1,0:T(8,128)S(1)} %get-tuple-element.62.pa, f32[8,3,3,512]{3,2,1,0:T(4,128)S(1)} %copy-done.9, ...), custom_call_target="tpu_custom_call" | custom-call | flops 20000000 | bytes 10792960 | tf_op jit(solution)/shard_map/pallas_call | solution.py:161
  123.8 3.9 %all-to-all-done.4 = f32[128,1,1536]{2,1,0:T(1,128)} async-done(((f32[128,1,1536]{2,1,0:T(1,128)}), f32[128,1,1536]{2,1,0:T(1,128)}, u32[]{:S(2)}, u32[]{:S(2)}) %all-to-all-start.4) | async-done | bytes 786464 | tf_op jit(solution)/shard_map/all_to_all | solution.py:497
  130.7 4.5 %shard_map.190 = (f32[3,96,512]{2,1,0:T(8,128)S(1)}, f32[3,96,512]{2,1,0:T(8,128)S(1)}, f32[16,96,128]{2,1,0:T(8,128)S(1)}) custom-call(s32[2]{0:T(128)S(1)} %copy-done.42, s32[3,512]{1,0:T(4,128)S(1)} %bitcast.42, s32[1,512]{1,0:T(1,128)S(1)} %copy-done.35, f32[1536,128]{1,0:T(8,128)} %bitcast.10.packed, f32[3,96,512]{2,1,0:T(8,128)S(1)} %copy-done.22, ...), custom_call_target="tpu_custom_call" | custom-call | flops 5000000000 | bytes 3497984 | tf_op jit(solution)/shard_map/pallas_call | solution.py:35
  136.3 2.8 shard_map.191
  139.2 17.1 %all_to_all.60.parts = f32[16,96,128]{2,1,0:T(8,128)S(1)} all-to-all(f32[16,96,128]{2,1,0:T(8,128)S(1)} %add.31), channel_id=1, replica_groups=mesh['net'=4,'z'=4,'y'=4,'core'=2] {'z','y'}, dimensions={0} | all-to-all | bytes 1572864 | tf_op jit(solution)/shard_map/all_to_all | solution.py:364
  156.4 16.0 %all_to_all.61.current = f32[16,96,128]{2,1,0:T(8,128)S(1)} all-to-all(f32[16,96,128]{2,1,0:T(8,128)S(1)} %shard_map.192), channel_id=1, replica_groups=mesh['net'=4,'z'=4,'y'=4,'core'=2] {'z','y'}, dimensions={0} | all-to-all | bytes 1572864 | tf_op jit(solution)/shard_map/all_to_all | solution.py:364
  173.0 2.2 collective-permute-start.6
  176.1 16.5 %all_to_all.62.volts = f32[16,96,128]{2,1,0:T(8,128)S(1)} all-to-all(f32[16,96,128]{2,1,0:T(8,128)S(1)} %get-tuple-element.46), channel_id=1, replica_groups=mesh['net'=4,'z'=4,'y'=4,'core'=2] {'z','y'}, dimensions={0} | all-to-all | bytes 1572864 | tf_op jit(solution)/shard_map/all_to_all | solution.py:364
  192.6 1.5 collective-permute-start.7
  194.0 2.0 shard_map.196.before
  196.0 3.2 %shard_map.197 = (f32[3,96,512]{2,1,0:T(8,128)S(1)}, f32[1536,128]{1,0:T(8,128)S(1)}) custom-call(s32[2]{0:T(128)S(1)} %copy-done.42, s32[3,512]{1,0:T(4,128)S(1)} %bitcast.45, s32[1,512]{1,0:T(1,128)S(1)} %copy-done.35, f32[16,96,128]{2,1,0:T(8,128)S(1)} %collective-permute-done.7.volts, f32[3,96,512]{2,1,0:T(8,128)S(1)} %shard_map.196.before, ...), custom_call_target="tpu_custom_call" | custom-call | flops 5000000000 | bytes 3352576 | tf_op jit(solution)/shard_map/pallas_call | solution.py:35
  200.9 5.2 %all-to-all-start.8 = ((f32[128,1,1536]{2,1,0:T(1,128)}), f32[128,1,1536]{2,1,0:T(1,128)}, u32[]{:S(2)}, u32[]{:S(2)}) async-start(f32[128,1,1536]{2,1,0:T(1,128)} %bitcast.34), calls=%async_computation.8 | async-start | bytes 1572864 | tf_op jit(solution)/shard_map/all_to_all | solution.py:497
  210.7 11.4 %all-to-all-done.8 = f32[128,1,1536]{2,1,0:T(1,128)} async-done(((f32[128,1,1536]{2,1,0:T(1,128)}), f32[128,1,1536]{2,1,0:T(1,128)}, u32[]{:S(2)}, u32[]{:S(2)}) %all-to-all-start.8) | async-done | bytes 786464 | tf_op jit(solution)/shard_map/all_to_all | solution.py:497
  223.2 5.0 %shard_map.199 = (f32[3,96,512]{2,1,0:T(8,128)}, f32[3,96,512]{2,1,0:T(8,128)S(1)}, f32[16,96,128]{2,1,0:T(8,128)S(1)}) custom-call(s32[2]{0:T(128)S(1)} %copy-done.43, s32[3,512]{1,0:T(4,128)S(1)} %bitcast.46, s32[1,512]{1,0:T(1,128)S(1)} %copy-done.36, f32[1536,128]{1,0:T(8,128)} %bitcast.12.packed, f32[3,96,512]{2,1,0:T(8,128)S(1)} %copy-done.20, ...), custom_call_target="tpu_custom_call" | custom-call | flops 5000000000 | bytes 3497984 | tf_op jit(solution)/shard_map/pallas_call | solution.py:35
  229.3 2.8 shard_map.200
  232.2 17.1 %all_to_all.63.parts = f32[16,96,128]{2,1,0:T(8,128)S(1)} all-to-all(f32[16,96,128]{2,1,0:T(8,128)S(1)} %add.32), channel_id=1, replica_groups=mesh['net'=4,'z'=4,'y'=4,'core'=2] {'z','y'}, dimensions={0} | all-to-all | bytes 1572864 | tf_op jit(solution)/shard_map/all_to_all | solution.py:364
  249.4 16.0 %all_to_all.64.current = f32[16,96,128]{2,1,0:T(8,128)S(1)} all-to-all(f32[16,96,128]{2,1,0:T(8,128)S(1)} %shard_map.201), channel_id=1, replica_groups=mesh['net'=4,'z'=4,'y'=4,'core'=2] {'z','y'}, dimensions={0} | all-to-all | bytes 1572864 | tf_op jit(solution)/shard_map/all_to_all | solution.py:364
  265.9 2.2 collective-permute-start.9
  269.7 16.5 %all_to_all.65.volts = f32[16,96,128]{2,1,0:T(8,128)S(1)} all-to-all(f32[16,96,128]{2,1,0:T(8,128)S(1)} %get-tuple-element.55), channel_id=1, replica_groups=mesh['net'=4,'z'=4,'y'=4,'core'=2] {'z','y'}, dimensions={0} | all-to-all | bytes 1572864 | tf_op jit(solution)/shard_map/all_to_all | solution.py:364
  287.6 2.0 shard_map.205.before
  289.6 2.8 shard_map.206
  (151 shorter events, 37.1 us)
Async XLA Ops:
  0.6 13.6 %copy-start.4 = (f32[1,4,3,96,512]{4,3,2,1,0:T(8,128)S(1)}, f32[1,4,3,96,512]{4,3,2,1,0:T(8,128)}, u32[]{:S(2)}) copy-start(f32[1,4,3,96,512]{4,3,2,1,0:T(8,128)} %param.33) | copy-start | bytes 7077892
  2.6 21.8 %all-to-all-start = ((f32[16,96,128]{2,1,0:T(8,128)}), f32[16,96,128]{2,1,0:T(8,128)S(1)}, u32[]{:S(2)}, u32[]{:S(2)}) async-start(f32[16,96,128]{2,1,0:T(8,128)} %broadcast_in_dim.39), calls=%async_computation | async-start | bytes 1572864 | tf_op jit(solution)/shard_map/all_to_all | solution.py:364
  14.2 2.0 copy-start
  16.2 2.0 copy-start.2
  18.9 7.7 %copy-start.54 = (s32[1,3,512]{2,0,1:T(1,128)S(1)}, s32[1,3,512]{2,0,1:T(1,128)}, u32[]{:S(2)}) copy-start(s32[1,3,512]{2,0,1:T(1,128)} %param.22) | copy-start | bytes 18436
  21.7 7.1 %copy-start.8 = (f32[8,3,3,512]{3,2,1,0:T(4,128)}, f32[8,3,3,512]{3,2,1,0:T(4,128)S(1)}, u32[]{:S(2)}) copy-start(f32[8,3,3,512]{3,2,1,0:T(4,128)S(1)} %get-tuple-element.33.coef) | copy-start | bytes 442372
  24.3 4.4 %collective-permute-start = (f32[16,96,128]{2,1,0:T(8,128)S(1)}, f32[16,96,128]{2,1,0:T(8,128)S(1)}, u32[]{:S(2)}, u32[]{:S(2)}) collective-permute-start(f32[16,96,128]{2,1,0:T(8,128)S(1)} %all-to-all-done.volts), channel_id=1, source_target_pairs={{0,1},{1,0},{2,3},{3,2},{4,5},{5,4},{6,7},{7,6},{8,9},{9,8},{10,11... | collective-permute-start | bytes 2359304 | tf_op jit(solution)/shard_map/ppermute | solution.py:368
  26.6 6.7 %copy-start.28 = (s32[1,3,512]{2,1,0:T(4,128)}, s32[1,3,512]{2,1,0:T(4,128)S(1)}, u32[]{:S(2)}) copy-start(s32[1,3,512]{2,1,0:T(4,128)S(1)} %copy.33) | copy-start | bytes 18436
  26.7 14.1 %copy-start.39 = (s32[2]{0:T(128)}, s32[2]{0:T(128)S(1)}, u32[]{:S(2)}) copy-start(s32[2]{0:T(128)S(1)} %pad_add_fusion.pos) | copy-start | bytes 28
  26.7 2.0 copy-start.45
  28.7 4.5 %copy-start.56 = (s32[96]{0:T(128)S(1)}, s32[96]{0:T(128)}, u32[]{:S(2)}) copy-start(s32[96]{0:T(128)} %param.20) | copy-start | bytes 1156
  28.7 4.5 %copy-start.55 = (f32[96]{0:T(128)S(1)}, f32[96]{0:T(128)}, u32[]{:S(2)}) copy-start(f32[96]{0:T(128)} %param.21) | copy-start | bytes 1156
  28.7 4.6 %copy-start.23 = (f32[1,96,128]{2,1,0:T(8,128)S(1)}, f32[1,96,128]{2,1,0:T(8,128)}, u32[]{:S(2)}) copy-start(f32[1,96,128]{2,1,0:T(8,128)} %param.18) | copy-start | bytes 147460
  28.7 4.6 %copy-start.50 = (f32[3,1,128]{2,1,0:T(1,128)S(1)}, f32[3,1,128]{2,1,0:T(1,128)}, u32[]{:S(2)}) copy-start(f32[3,1,128]{2,1,0:T(1,128)} %source.5) | copy-start | bytes 4612
  33.0 3.2 %copy-start.52 = (f32[3,96,512]{2,1,0:T(8,128)}, f32[3,96,512]{2,1,0:T(8,128)S(1)}, u32[]{:S(2)}) copy-start(f32[3,96,512]{2,1,0:T(8,128)S(1)} %get-tuple-element.34.h) | copy-start | bytes 1769476
  33.0 3.2 %collective-permute-start.1 = (f32[16,96,128]{2,1,0:T(8,128)S(1)}, f32[16,96,128]{2,1,0:T(8,128)S(1)}, u32[]{:S(2)}, u32[]{:S(2)}) collective-permute-start(f32[16,96,128]{2,1,0:T(8,128)S(1)} %get-tuple-element.35), channel_id=1, source_target_pairs={{0,1},{1,0},{2,3},{3,2},{4,5},{5,4},{6,7},{7,6},{8,9},{9,8},{10,11... | collective-permute-start | bytes 2359304 | tf_op jit(solution)/shard_map/ppermute | solution.py:368
  37.1 17.4 %all-to-all-start.1 = ((f32[16,96,128]{2,1,0:T(8,128)}), f32[16,96,128]{2,1,0:T(8,128)S(1)}, u32[]{:S(2)}, u32[]{:S(2)}) async-start(f32[16,96,128]{2,1,0:T(8,128)} %add.30), calls=%async_computation.1 | async-start | bytes 1572864 | tf_op jit(solution)/shard_map/all_to_all | solution.py:364
  44.2 15.1 %collective-permute-start.2 = (f32[128,2048]{1,0:T(8,128)}, f32[128,2048]{1,0:T(8,128)}, u32[]{:S(2)}, u32[]{:S(2)}) collective-permute-start(f32[128,2048]{1,0:T(8,128)} %get-tuple-element.37), channel_id=1, source_target_pairs={{0,1},{1,0},{2,3},{3,2},{4,5},{5,4},{6,7},{7,6},{8,9},{9,8},{10,11... | collective-permute-start | bytes 3145736 | tf_op jit(solution)/shard_map/ppermute | solution.py:368
  55.5 16.4 %all-to-all-start.2 = ((f32[16,96,128]{2,1,0:T(8,128)}), f32[16,96,128]{2,1,0:T(8,128)S(1)}, u32[]{:S(2)}, u32[]{:S(2)}) async-start(f32[16,96,128]{2,1,0:T(8,128)} %copy-done.6), calls=%async_computation.2 | async-start | bytes 1572864 | tf_op jit(solution)/shard_map/all_to_all | solution.py:364
  72.5 3.5 %collective-permute-start.3 = (f32[96,128]{1,0:T(8,128)S(1)}, f32[96,128]{1,0:T(8,128)S(1)}, u32[]{:S(2)}, u32[]{:S(2)}) collective-permute-start(f32[96,128]{1,0:T(8,128)S(1)} %shard_map.184), channel_id=1, source_target_pairs={{0,1},{1,0},{2,3},{3,2},{4,5},{5,4},{6,7},{7,6},{8,9},{9,8},{10,11... | collective-permute-start | bytes 147464 | tf_op jit(solution)/shard_map/ppermute | solution.py:368
  77.6 17.4 %all-to-all-start.3 = ((f32[16,96,128]{2,1,0:T(8,128)}), f32[16,96,128]{2,1,0:T(8,128)S(1)}, u32[]{:S(2)}, u32[]{:S(2)}) async-start(f32[16,96,128]{2,1,0:T(8,128)} %copy-done.12), calls=%async_computation.3 | async-start | bytes 1572864 | tf_op jit(solution)/shard_map/all_to_all | solution.py:364
  95.0 6.7 %collective-permute-start.4 = (f32[16,96,128]{2,1,0:T(8,128)S(1)}, f32[16,96,128]{2,1,0:T(8,128)S(1)}, u32[]{:S(2)}, u32[]{:S(2)}) collective-permute-start(f32[16,96,128]{2,1,0:T(8,128)S(1)} %all-to-all-done.3.volts), channel_id=1, source_target_pairs={{0,1},{1,0},{2,3},{3,2},{4,5},{5,4},{6,7},{7,6},{8,9},{9,8},{10,11... | collective-permute-start | bytes 2359304 | tf_op jit(solution)/shard_map/ppermute | solution.py:368
  97.2 4.6 %copy-start.34 = (s32[1,512]{1,0:T(1,128)}, s32[1,512]{1,0:T(1,128)S(1)}, u32[]{:S(2)}) copy-start(s32[1,512]{1,0:T(1,128)S(1)} %add_select_fusion.places) | copy-start | bytes 6148
  99.8 2.0 copy-start.37
  99.8 2.0 copy-start.30
  99.8 2.0 copy-start.41
  99.8 2.0 copy-start.53
  101.8 9.8 %copy-start.9 = (f32[8,3,3,512]{3,2,1,0:T(4,128)S(1)}, f32[8,3,3,512]{3,2,1,0:T(4,128)}, u32[]{:S(2)}) copy-start(f32[8,3,3,512]{3,2,1,0:T(4,128)} %copy-done.8) | copy-start | bytes 442372
  105.9 21.8 %all-to-all-start.4 = ((f32[128,1,1536]{2,1,0:T(1,128)}), f32[128,1,1536]{2,1,0:T(1,128)}, u32[]{:S(2)}, u32[]{:S(2)}) async-start(f32[128,1,1536]{2,1,0:T(1,128)} %bitcast.33), calls=%async_computation.4 | async-start | bytes 1572864 | tf_op jit(solution)/shard_map/all_to_all | solution.py:497
  111.6 2.0 copy-start.1
  113.6 2.0 copy-start.3
  130.7 5.6 %copy-start.47 = (f32[96,128]{1,0:T(8,128)S(1)}, f32[96,128]{1,0:T(8,128)}, u32[]{:S(2)}) copy-start(f32[96,128]{1,0:T(8,128)} %copy-done.46) | copy-start | bytes 147460
  130.7 5.6 %copy-start.51 = (f32[3,1,128]{2,1,0:T(1,128)S(1)}, f32[3,1,128]{2,1,0:T(1,128)}, u32[]{:S(2)}) copy-start(f32[3,1,128]{2,1,0:T(1,128)} %source.5) | copy-start | bytes 4612
  135.2 3.9 %copy-start.15 = (f32[3,96,512]{2,1,0:T(8,128)}, f32[3,96,512]{2,1,0:T(8,128)S(1)}, u32[]{:S(2)}) copy-start(f32[3,96,512]{2,1,0:T(8,128)S(1)} %get-tuple-element.50.a1) | copy-start | bytes 1769476
  135.2 3.9 %collective-permute-start.5 = (f32[16,96,128]{2,1,0:T(8,128)S(1)}, f32[16,96,128]{2,1,0:T(8,128)S(1)}, u32[]{:S(2)}, u32[]{:S(2)}) collective-permute-start(f32[16,96,128]{2,1,0:T(8,128)S(1)} %get-tuple-element.45), channel_id=1, source_target_pairs={{0,1},{1,0},{2,3},{3,2},{4,5},{5,4},{6,7},{7,6},{8,9},{9,8},{10,11... | collective-permute-start | bytes 2359304 | tf_op jit(solution)/shard_map/ppermute | solution.py:368
  173.0 3.1 %collective-permute-start.6 = (f32[96,128]{1,0:T(8,128)S(1)}, f32[96,128]{1,0:T(8,128)S(1)}, u32[]{:S(2)}, u32[]{:S(2)}) collective-permute-start(f32[96,128]{1,0:T(8,128)S(1)} %shard_map.194), channel_id=1, source_target_pairs={{0,1},{1,0},{2,3},{3,2},{4,5},{5,4},{6,7},{7,6},{8,9},{9,8},{10,11... | collective-permute-start | bytes 147464 | tf_op jit(solution)/shard_map/ppermute | solution.py:368
  176.1 16.5 %copy-start.48 = (f32[96,128]{1,0:T(8,128)}, f32[96,128]{1,0:T(8,128)S(1)}, u32[]{:S(2)}) copy-start(f32[96,128]{1,0:T(8,128)S(1)} %get-tuple-element.52.volts) | copy-start | bytes 147460
  192.6 3.4 %copy-start.38 = (f32[1,512]{1,0:T(1,128)S(1)}, f32[1,512]{1,0:T(1,128)}, u32[]{:S(2)}) copy-start(f32[1,512]{1,0:T(1,128)} %copy-done.37) | copy-start | bytes 6148
  192.6 3.4 %collective-permute-start.7 = (f32[16,96,128]{2,1,0:T(8,128)S(1)}, f32[16,96,128]{2,1,0:T(8,128)S(1)}, u32[]{:S(2)}, u32[]{:S(2)}) collective-permute-start(f32[16,96,128]{2,1,0:T(8,128)S(1)} %all_to_all.62.volts), channel_id=1, source_target_pairs={{0,1},{1,0},{2,3},{3,2},{4,5},{5,4},{6,7},{7,6},{8,9},{9,8},{10,11... | collective-permute-start | bytes 2359304 | tf_op jit(solution)/shard_map/ppermute | solution.py:368
  200.9 21.3 %copy-start.32 = (s32[1,3,512]{2,1,0:T(4,128)S(1)}, s32[1,3,512]{2,1,0:T(4,128)}, u32[]{:S(2)}) copy-start(s32[1,3,512]{2,1,0:T(4,128)} %copy-done.28) | copy-start | bytes 18436
  200.9 21.3 %copy-start.36 = (s32[1,512]{1,0:T(1,128)S(1)}, s32[1,512]{1,0:T(1,128)}, u32[]{:S(2)}) copy-start(s32[1,512]{1,0:T(1,128)} %copy-done.34) | copy-start | bytes 6148
  200.9 21.3 %copy-start.43 = (s32[2]{0:T(128)S(1)}, s32[2]{0:T(128)}, u32[]{:S(2)}) copy-start(s32[2]{0:T(128)} %copy-done.39) | copy-start | bytes 28
  200.9 21.3 %all-to-all-start.8 = ((f32[128,1,1536]{2,1,0:T(1,128)}), f32[128,1,1536]{2,1,0:T(1,128)}, u32[]{:S(2)}, u32[]{:S(2)}) async-start(f32[128,1,1536]{2,1,0:T(1,128)} %bitcast.34), calls=%async_computation.8 | async-start | bytes 1572864 | tf_op jit(solution)/shard_map/all_to_all | solution.py:497
  223.2 6.1 %copy-start.49 = (f32[96,128]{1,0:T(8,128)S(1)}, f32[96,128]{1,0:T(8,128)}, u32[]{:S(2)}) copy-start(f32[96,128]{1,0:T(8,128)} %copy-done.48) | copy-start | bytes 147460
  228.2 3.8 %collective-permute-start.8 = (f32[16,96,128]{2,1,0:T(8,128)S(1)}, f32[16,96,128]{2,1,0:T(8,128)S(1)}, u32[]{:S(2)}, u32[]{:S(2)}) collective-permute-start(f32[16,96,128]{2,1,0:T(8,128)S(1)} %get-tuple-element.53), channel_id=1, source_target_pairs={{0,1},{1,0},{2,3},{3,2},{4,5},{5,4},{6,7},{7,6},{8,9},{9,8},{10,11... | collective-permute-start | bytes 2359304 | tf_op jit(solution)/shard_map/ppermute | solution.py:368
  265.9 3.1 %collective-permute-start.9 = (f32[96,128]{1,0:T(8,128)S(1)}, f32[96,128]{1,0:T(8,128)S(1)}, u32[]{:S(2)}, u32[]{:S(2)}) collective-permute-start(f32[96,128]{1,0:T(8,128)S(1)} %shard_map.203), channel_id=1, source_target_pairs={{0,1},{1,0},{2,3},{3,2},{4,5},{5,4},{6,7},{7,6},{8,9},{9,8},{10,11... | collective-permute-start | bytes 147464 | tf_op jit(solution)/shard_map/ppermute | solution.py:368
  286.1 3.4 %copy-start.33 = (f32[1,512]{1,0:T(1,128)S(1)}, f32[1,512]{1,0:T(1,128)}, u32[]{:S(2)}) copy-start(f32[1,512]{1,0:T(1,128)} %get-tuple-element.57.surge) | copy-start | bytes 6148
  286.1 3.4 %collective-permute-start.10 = (f32[16,96,128]{2,1,0:T(8,128)S(1)}, f32[16,96,128]{2,1,0:T(8,128)S(1)}, u32[]{:S(2)}, u32[]{:S(2)}) collective-permute-start(f32[16,96,128]{2,1,0:T(8,128)S(1)} %all_to_all.65.volts), channel_id=1, source_target_pairs={{0,1},{1,0},{2,3},{3,2},{4,5},{5,4},{6,7},{7,6},{8,9},{9,8},{10,11... | collective-permute-start | bytes 2359304 | tf_op jit(solution)/shard_map/ppermute | solution.py:368
  (26 other events, 23.9 us)
where the time goes:
time: 294 us; the launch traced here: 292 us
  blocking collectives  99.2 us (34%)
  waiting for transfers between devices  52.7 us (18%)
  Pallas kernels  52.2 us (18%)
  starting transfers between devices  46.8 us (16%)
  local copies, waits for them, and re-layouts  33.9 us (12%)
  other arithmetic  6.2 us (2%)
    all_to_all x6, blocking collectives, exchanged(): return lax.all_to_all(x, PLANE, 0, 0, tiled=True)  99.2 us
    pallas_call x29, Pallas kernels, call(): pl.pallas_call(kernel, out_shape=outs, in_specs=[SMEM] * len(scalars) + [...  47.1 us
    all_to_all x4, waiting for transfers between devices, exchanged(): return lax.all_to_all(x, PLANE, 0, 0, tiled=True)  36.3 us
    unnamed x117, local copies, waits for them, and re-layouts  31.9 us
    all_to_all x4, starting transfers between devices, exchanged(): return lax.all_to_all(x, PLANE, 0, 0, tiled=True)  19.5 us
    ppermute x11, starting transfers between devices, swapped(): return lax.ppermute(x, 'core', [(0, 1), (1, 0)])  16.5 us
    all_to_all x2, waiting for transfers between devices, on_device(): packed = lax.all_to_all(packed, NET_LINE, 0, 0, tiled=True)  15.3 us
    all_to_all x2, starting transfers between devices, on_device(): packed = lax.all_to_all(packed, NET_LINE, 0, 0, tiled=True)  10.9 us
  transfers between devices with their start and end apart: 17, of which 9 were waited for; matrix products, arithmetic and copies ran while one was open for 2% of the time, Pallas kernels for 9%

commit v1 on v0

--- a/solution.py
+++ b/solution.py
@@ -13,6 +13,7 @@
 LINE = ("z", "y", "core")
 NET_LINE = ("net", "z", "y", "core")
 SIDE = 4
+SURGE = 2 * STEPS + 2
 CHIPS = SIDE * SIDE
 CAPACITY = 5
 F32 = jnp.float32
@@ -74,6 +75,14 @@
     return lax.dot_general(a, b, (dims, ((), ())), preferred_element_type=F32)
 
 
+def own_core():
+    return lax.axis_index("core")
+
+
+def own_chip():
+    return lax.axis_index("z") * SIDE + lax.axis_index("y")
+
+
 NN = ((1,), (0,))
 NT = ((1,), (1,))
 TN = ((0,), (0,))
@@ -86,9 +95,14 @@
     ]
 
 
-def lag_coefficients(own, delay, pw, rw, pa, ra, coef):
+def lag_coefficients(own, delay, surge, pw, rw, pa, ra, coef):
     live = own[...]
     steps = delay[...]
+    coef[SURGE, 0, 0:1] = surge[...] * live
+    coef[SURGE, 0, 1:2] = 2.0 * surge[...] * live
+    coef[SURGE, 0, 2:3] = live
+    for p in (1, 2):
+        coef[SURGE, p] = jnp.zeros(coef.shape[2:], F32)
     first = (steps == 1).astype(F32)
     second = (steps == 2).astype(F32)
     for p in range(3):
@@ -139,10 +153,10 @@
             out[p] = value
 
 
-def fold_first(own, delay, pw, rw, pa, ra, xw, xa, hist, out, coef):
+def fold_first(own, delay, surge, pw, rw, pa, ra, xw, xa, hist, out, coef):
     @pl.when(pl.program_id(0) == 0)
     def _():
-        lag_coefficients(own, delay, pw, rw, pa, ra, coef)
+        lag_coefficients(own, delay, surge, pw, rw, pa, ra, coef)
 
     fold_states((0,), own, delay, pw, pa, coef, xw, xa, hist, (out,))
 
@@ -170,15 +184,15 @@
     )(*small, *states)
 
 
-def cut_kernel(pos, inverse, mine, give):
+def cut_kernel(inverse, mine, give):
     rows = inverse.shape[0]
     for k in range(CHIPS):
         lanes = slice(k * 128, (k + 1) * 128)
-        start = pl.multiple_of((k * 2 + pos[0]) * 128, 128)
+        start = pl.multiple_of((k * 2 + own_core()) * 128, 128)
         high, low = halves(inverse[:, pl.ds(start, 128)])
         mine[0:rows, lanes] = high
         mine[rows : 2 * rows, lanes] = low
-        start = pl.multiple_of((k * 2 + 1 - pos[0]) * 128, 128)
+        start = pl.multiple_of((k * 2 + 1 - own_core()) * 128, 128)
         give[:, lanes] = inverse[:, pl.ds(start, 128)]
 
 
@@ -208,18 +222,18 @@
             emit(p, cut, both[:scenarios] + both[scenarios:])
 
 
-def gather_kernel(pos, terminal, volts, out, split):
+def gather_kernel(terminal, volts, out, split):
     def emit(p, cut, value):
         out[p, :, cut] = value
 
-    gather_into(pos[0], terminal, volts, split, emit)
-
-
-def gather_rest(pos, terminal, volts, before, out, split):
+    gather_into(own_core(), terminal, volts, split, emit)
+
+
+def gather_rest(terminal, volts, before, out, split):
     def emit(p, cut, value):
         out[p, :, cut] = before[p, :, cut] + value
 
-    gather_into(1 - pos[0], terminal, volts, split, emit)
+    gather_into(1 - own_core(), terminal, volts, split, emit)
 
 
 def scatter_into(side, terminal, split, emit):
@@ -242,29 +256,28 @@
     return jnp.concatenate(parts, axis=1)
 
 
-def scatter_other(pos, terminal, h, out, split):
+def scatter_other(terminal, h, ends, out):
     def emit(k, value):
         out[k] = value
 
-    split[...] = split_ends(h)
-    scatter_into(1 - pos[0], terminal, split[...], emit)
-
-
-def first_kernel(pos, terminal, volts, before, base, coef, term, h_out, out, split, ends):
-    gather_rest(pos, terminal, volts, before, term, split)
+    ends[...] = split_ends(h)
+    scatter_into(1 - own_core(), terminal, ends[...], emit)
+
+
+def first_kernel(terminal, volts, before, base, coef, term, h_out, ends, out, split):
+    gather_rest(terminal, volts, before, term, split)
     drop = mix(coef[0], term)
     for p in range(3):
         h_out[p] = base[p] - drop[p]
-    scatter_other(pos, terminal, h_out, out, ends)
-
-
-def scatter_mine(step, pos, terminal, h, source, drain, volts, out, split):
+    scatter_other(terminal, h_out, ends, out)
+
+
+def scatter_mine(step, terminal, ends, source, drain, volts, out):
     def emit(k, value):
         out[k] = value
 
-    split[...] = split_ends(h)
-    scatter_into(pos[0], terminal, split[...], emit)
-    me = pos[1]
+    scatter_into(own_core(), terminal, ends[...], emit)
+    me = own_chip()
     out[me] = out[me] + source[step] - drain[...] * volts[...]
 
 
@@ -277,14 +290,15 @@
     return -(-CAPACITY * values // 128)
 
 
-def pack_kernel(pos, terminal, places, volts, before, surge2, h, term, packed, split):
-    gather_rest(pos, terminal, volts, before, term, split)
-    waves = [surge2[...] * term[p] - h[p] for p in range(3)]
+def pack_kernel(terminal, volts, before, coef, h, term, packed, split):
+    gather_rest(terminal, volts, before, term, split)
+    surge2 = coef[SURGE, 0, 1:2, :]
+    waves = [surge2 * term[p] - h[p] for p in range(3)]
     high, low = halves(jnp.concatenate(waves, axis=0))
     lines = packed_lines(high.shape[0])
     owners = packed.shape[0] // lines
     rows = []
-    for hot in hot_places(places[...], owners):
+    for hot in hot_places(terminal[3:4, :], owners):
         rows.append(dot(hot, high, NT) + dot(hot, low, NT))
     used = sum(r.shape[1] for r in rows)
     rows.append(jnp.zeros((owners, lines * 128 - used), F32))
@@ -306,7 +320,7 @@
         out[p] = base[p] - a[p] - b[p] - c[p] + d[p]
 
 
-def arrive_kernel(pos, terminal, places, packed, base, coef, arrived, h_out, out, ends):
+def arrive_kernel(terminal, packed, base, coef, arrived, h_out, ends, out):
     scenarios = base.shape[1]
     wide = 3 * scenarios
     lines = packed_lines(wide)
@@ -315,7 +329,7 @@
         [packed[pl.ds(k, owners, stride=lines), :] for k in range(lines)], axis=1
     )
     total = None
-    for r, hot in enumerate(hot_places(places[...], owners)):
+    for r, hot in enumerate(hot_places(terminal[3:4, :], owners)):
         high, low = halves(rows[:, r * wide : (r + 1) * wide])
         part = dot(high, hot, TN) + dot(low, hot, TN)
         total = part if total is None else total + part
@@ -324,15 +338,17 @@
     gain = mix(coef[STEPS], arrived)
     for p in range(3):
         h_out[p] = base[p] + gain[p]
-    scatter_other(pos, terminal, h_out, out, ends)
-
-
-def last_kernel(pos, terminal, volts, before, surge, h, out, split):
+    scatter_other(terminal, h_out, ends, out)
+
+
+def last_kernel(terminal, volts, before, coef, h, out, split):
+    surge = coef[SURGE, 0, 0:1, :]
+
     def emit(p, cut, value):
         term = before[p, :, cut] + value
         out[p, :, cut] = surge[:, cut] * term - h[p, :, cut]
 
-    gather_into(1 - pos[0], terminal, volts, split, emit)
+    gather_into(1 - own_core(), terminal, volts, split, emit)
 
 
 def total_kernel(parts, out):
@@ -406,34 +422,31 @@
     )
     rank = jnp.sum(earlier.astype(jnp.int32), axis=0)
     places = jnp.where(live, partners * 8 + rank, -1)[None]
-    terminal = terminal_node[0]
-    surge = surge_conductance * live_float
-    surge2 = 2.0 * surge
+    table = jnp.concatenate([terminal_node[0], places], axis=0)
     lane = jnp.arange(rows, dtype=jnp.int32)[None]
     first_node = net * node_count + me * rows
     drain = jnp.where(
         fault_node[:, None] - first_node == lane, fault_conductance[:, None], 0.0
     )
-    pos = jnp.stack([core, z * SIDE + y]).astype(jnp.int32)
 
     half = shape(CHIPS, scenarios, rows)
     waves = shape(3, scenarios, slots)
     splits = pltpu.VMEM((2 * scenarios, 16 * rows), BF16)
-    end_split = pltpu.VMEM((2 * scenarios, ends), BF16)
+    end_split = shape(2 * scenarios, ends, dtype=BF16)
 
     block = shape(scenarios, rows)
 
     def first_gather(plane):
-        return call(gather_kernel, (pos,), (terminal, plane), waves, [splits], 4_000_000_000)
-
-    def solve(h, other, step, voltage_rows):
+        return call(gather_kernel, (), (table, plane), waves, [splits], 4_000_000_000)
+
+    def solve(ends_split, other, step, voltage_rows):
         sent = swapped(other)
         mine = call(
             functools.partial(scatter_mine, step),
-            (pos,),
-            (terminal, h, sources, drain, voltage_rows),
+            (),
+            (table, ends_split, sources, drain, voltage_rows),
             half,
-            [end_split],
+            (),
             4_000_000_000,
         )
         plane = exchanged(call(total_kernel, (), (exchanged(mine + sent),), half))
@@ -449,16 +462,24 @@
     live_row, delays, poles_w, poles_a = small
     base_0, coef = fold(
         fold_first,
-        (live_row, delays, poles_w, residue_wave[0], poles_a, residue_admit[0]),
+        (
+            live_row,
+            delays,
+            surge_conductance,
+            poles_w,
+            residue_wave[0],
+            poles_a,
+            residue_admit[0],
+        ),
         states,
         1,
-        [shape(2 * STEPS + 2, 3, 3, slots)],
-    )
-    plane, base_0, coef = lax.optimization_barrier((plane, base_0, coef))
+        [shape(SURGE + 1, 3, 3, slots)],
+    )
+    plane, base_0, coef, table = lax.optimization_barrier((plane, base_0, coef, table))
     base = [base_0, *fold(fold_later, (*small, coef), states, STEPS - 1, [])]
     inverse_mine, give = call(
         cut_kernel,
-        (pos,),
+        (),
         (conductance_inverse[0],),
         (shape(2 * rows, CHIPS * 128, dtype=BF16), shape(rows, CHIPS * 128)),
     )
@@ -467,15 +488,15 @@
     )
     far = swapped(plane)
     before = first_gather(plane)
-    t0, h, other = call(
+    t0, h, ends_split, other = call(
         first_kernel,
-        (pos,),
-        (terminal, far, before, base[0], coef),
-        (waves, waves, half),
-        [splits, end_split],
+        (),
+        (table, far, before, base[0], coef),
+        (waves, waves, end_split, half),
+        [splits],
         8_000_000_000,
     )
-    voltage_rows, copies = solve(h, other, 0, voltage_rows)
+    voltage_rows, copies = solve(ends_split, other, 0, voltage_rows)
     terms = [t0]
     arrivals = []
     lines = packed_lines(3 * scenarios)
@@ -486,8 +507,8 @@
         before = first_gather(plane)
         term, packed = call(
             pack_kernel,
-            (pos,),
-            (terminal, places, far, before, surge2, h),
+            (),
+            (table, far, before, coef, h),
             (waves, packed_shape),
             [splits],
             5_000_000_000,
@@ -497,21 +518,21 @@
         packed = lax.all_to_all(packed, NET_LINE, 0, 0, tiled=True)
         packed = packed.reshape(devices * lines, 128)
         known = call((known_1, known_2)[step - 1], (), (base[step], coef, *terms, *arrivals), waves)
-        arrived, h, other = call(
+        arrived, h, ends_split, other = call(
             arrive_kernel,
-            (pos,),
-            (terminal, places, packed, known, coef),
-            (waves, waves, half),
-            [end_split],
+            (),
+            (table, packed, known, coef),
+            (waves, waves, end_split, half),
+            (),
             5_000_000_000,
         )
         arrivals.append(arrived)
-        voltage_rows, copies = solve(h, other, step, voltage_rows)
+        voltage_rows, copies = solve(ends_split, other, step, voltage_rows)
     plane = exchanged(copies)
     far = swapped(plane)
     before = first_gather(plane)
     current = call(
-        last_kernel, (pos,), (terminal, far, before, surge, h), waves, [splits], 4_000_000_000
+        last_kernel, (), (table, far, before, coef, h), waves, [splits], 4_000_000_000
     )
     return voltage_rows[None], current[None]
 

time: 294 us -> 290 us (0.986)
  blocking collectives: 99.2 us -> 116 us
  waiting for transfers between devices: 52.7 us -> 40.4 us
  other arithmetic: 6.2 us -> 2.18 us
  Pallas kernels: 52.2 us -> 49.2 us
    all_to_all x6 -> x7, blocking collectives: 99.2 us -> 116 us  [exchanged(): return lax.all_to_all(x, PLANE, 0, 0, tiled=True)]
    all_to_all x4 -> x3, waiting for transfers between devices: 36.3 us -> 22.4 us  [exchanged(): return lax.all_to_all(x, PLANE, 0, 0, tiled=True)]
    pallas_call x29, Pallas kernels: 47.1 us -> 44.1 us  [call(): pl.pallas_call(kernel, out_shape=outs, in_specs=[SMEM] * len(scalars) + [...]
    all_to_all x4 -> x3, starting transfers between devices: 19.5 us -> 17 us  [exchanged(): return lax.all_to_all(x, PLANE, 0, 0, tiled=True)]
    unnamed x117 -> x99, local copies, waits for them, and re-layouts: 31.9 us -> 32.6 us
  transfers between devices with their start and end apart: 17 -> 16, of which waited for: 9 -> 11; matrix products, arithmetic and copies ran while one was open for 2% -> 1% of each run, Pallas kernels for 9% -> 8%
where the time goes in v1:
time: 290 us; the launch traced here: 288 us
  blocking collectives  116 us (40%)
  Pallas kernels  49.2 us (17%)
  starting transfers between devices  44 us (15%)
  waiting for transfers between devices  40.4 us (14%)
  local copies, waits for them, and re-layouts  34.6 us (12%)
    all_to_all x7, blocking collectives, exchanged(): return lax.all_to_all(x, PLANE, 0, 0, tiled=True)  116 us
    pallas_call x29, Pallas kernels, call(): pl.pallas_call(kernel, out_shape=outs, in_specs=[SMEM] * len(scalars) + [...  44.1 us
    unnamed x99, local copies, waits for them, and re-layouts  32.6 us
    all_to_all x3, waiting for transfers between devices, exchanged(): return lax.all_to_all(x, PLANE, 0, 0, tiled=True)  22.4 us
    all_to_all x3, starting transfers between devices, exchanged(): return lax.all_to_all(x, PLANE, 0, 0, tiled=True)  17 us
    ppermute x11, starting transfers between devices, swapped(): return lax.ppermute(x, 'core', [(0, 1), (1, 0)])  16.5 us
    all_to_all x2, waiting for transfers between devices, on_device(): packed = lax.all_to_all(packed, NET_LINE, 0, 0, tiled=True)  15.2 us
    all_to_all x2, starting transfers between devices, on_device(): packed = lax.all_to_all(packed, NET_LINE, 0, 0, tiled=True)  10.6 us
  transfers between devices with their start and end apart: 16, of which 11 were waited for; matrix products, arithmetic and copies ran while one was open for 1% of the time, Pallas kernels for 8%

profile of v1, /device:TPU:1, one launch (start us, length us, event | category | flops | bytes accessed | tf_op | source)
XLA Modules:
  0.0 288.0 jit_solution(13221450664656951378)
XLA Ops:
  0.6 2.0 broadcast_in_dim.38
  2.6 8.6 %all-to-all-start = ((f32[16,96,128]{2,1,0:T(8,128)}), f32[16,96,128]{2,1,0:T(8,128)S(1)}, u32[]{:S(2)}, u32[]{:S(2)}) async-start(f32[16,96,128]{2,1,0:T(8,128)} %broadcast_in_dim.38), calls=%async_computation | async-start | bytes 1572864 | tf_op jit(solution)/shard_map/all_to_all | solution.py:380
  14.4 2.0 copy-done
  16.4 2.0 copy-done.2
  19.8 1.9 shard_map.176
  22.8 1.6 all-to-all-done.volts
  24.4 2.3 collective-permute-start
  26.7 1.4 shard_map.177.before
  28.7 4.8 %shard_map.178 = (f32[3,96,512]{2,1,0:T(8,128)S(1)}, f32[3,96,512]{2,1,0:T(8,128)S(1)}, bf16[192,1536]{1,0:T(8,128)(2,1)S(1)}, f32[16,96,128]{2,1,0:T(8,128)S(1)}) custom-call(s32[4,512]{1,0:T(4,128)S(1)} %pad_add_fusion.terminal, f32[16,96,128]{2,1,0:T(8,128)} %collective-permute-done.volts, f32[3,96,512]{2,1,0:T(8,128)S(1)} %shard_map.177.before, ...), custom_call_target="tpu_custom_call" | custom-call | flops 8000000000 | bytes 4696064 | tf_op jit(solution)/shard_map/pallas_call | solution.py:36
  34.1 2.2 shard_map.179
  37.4 4.1 %all-to-all-start.1 = ((f32[16,96,128]{2,1,0:T(8,128)}), f32[16,96,128]{2,1,0:T(8,128)S(1)}, u32[]{:S(2)}, u32[]{:S(2)}) async-start(f32[16,96,128]{2,1,0:T(8,128)} %add.26), calls=%async_computation.1 | async-start | bytes 1572864 | tf_op jit(solution)/shard_map/all_to_all | solution.py:380
  41.4 1.6 copy-done.15
  43.0 1.3 shard_map.181
  45.7 9.5 %all-to-all-done.1.parts = f32[16,96,128]{2,1,0:T(8,128)S(1)} async-done(((f32[16,96,128]{2,1,0:T(8,128)}), f32[16,96,128]{2,1,0:T(8,128)S(1)}, u32[]{:S(2)}, u32[]{:S(2)}) %all-to-all-start.1) | async-done | bytes 786464 | tf_op jit(solution)/shard_map/all_to_all | solution.py:380
  56.2 4.3 %all-to-all-start.2 = ((f32[16,96,128]{2,1,0:T(8,128)}), f32[16,96,128]{2,1,0:T(8,128)}, u32[]{:S(2)}, u32[]{:S(2)}) async-start(f32[16,96,128]{2,1,0:T(8,128)} %copy-done.8), calls=%async_computation.2 | async-start | bytes 1572864 | tf_op jit(solution)/shard_map/all_to_all | solution.py:380
  60.5 1.4 shard_map.183.inverse
  61.9 11.3 %all-to-all-done.2.current = f32[16,96,128]{2,1,0:T(8,128)} async-done(((f32[16,96,128]{2,1,0:T(8,128)}), f32[16,96,128]{2,1,0:T(8,128)}, u32[]{:S(2)}, u32[]{:S(2)}) %all-to-all-start.2) | async-done | bytes 786464 | tf_op jit(solution)/shard_map/all_to_all | solution.py:380
  73.2 1.6 shard_map.184
  74.8 2.7 collective-permute-start.3
  78.8 1.7 shard_map.182.a
  80.5 17.0 %all_to_all.60.volts = f32[16,96,128]{2,1,0:T(8,128)S(1)} all-to-all(f32[16,96,128]{2,1,0:T(8,128)S(1)} %get-tuple-element.43), channel_id=1, replica_groups=mesh['net'=4,'z'=4,'y'=4,'core'=2] {'z','y'}, dimensions={0} | all-to-all | bytes 1572864 | tf_op jit(solution)/shard_map/all_to_all | solution.py:380
  98.6 1.4 shard_map.186.before
  100.5 2.6 shard_map.187
  104.9 5.8 %all-to-all-start.4 = ((f32[128,1,1536]{2,1,0:T(1,128)}), f32[128,1,1536]{2,1,0:T(1,128)}, u32[]{:S(2)}, u32[]{:S(2)}) async-start(f32[128,1,1536]{2,1,0:T(1,128)} %bitcast.31), calls=%async_computation.4 | async-start | bytes 1572864 | tf_op jit(solution)/shard_map/all_to_all | solution.py:518
  110.7 2.0 copy-done.1
  112.7 2.0 copy-done.3
  115.6 3.2 %shard_map.188 = (f32[3,96,512]{2,1,0:T(8,128)S(1)}, f32[3,96,512]{2,1,0:T(8,128)S(1)}) custom-call(f32[1,512]{1,0:T(1,128)S(1)} %get-tuple-element.65.own, s32[1,512]{1,0:T(1,128)S(1)} %copy-done.36, f32[6,512]{1,0:T(8,128)S(1)} %get-tuple-element.69.pw, f32[6,512]{1,0:T(8,128)S(1)} %get-tuple-element.68.pa, f32[9,3,3,512]{3,2,1,0:T(4,128)S(1)} %copy-done.18, ...), custom_call_target="tpu_custom_call" | custom-call | flops 20000000 | bytes 10811392 | tf_op jit(solution)/shard_map/pallas_call | solution.py:175
  120.0 6.7 %all-to-all-done.4 = f32[128,1,1536]{2,1,0:T(1,128)} async-done(((f32[128,1,1536]{2,1,0:T(1,128)}), f32[128,1,1536]{2,1,0:T(1,128)}, u32[]{:S(2)}, u32[]{:S(2)}) %all-to-all-start.4) | async-done | bytes 786464 | tf_op jit(solution)/shard_map/all_to_all | solution.py:518
  127.7 4.5 %shard_map.190 = (f32[3,96,512]{2,1,0:T(8,128)S(1)}, f32[3,96,512]{2,1,0:T(8,128)S(1)}, bf16[192,1536]{1,0:T(8,128)(2,1)S(1)}, f32[16,96,128]{2,1,0:T(8,128)S(1)}) custom-call(s32[4,512]{1,0:T(4,128)S(1)} %pad_add_fusion.terminal, f32[1536,128]{1,0:T(8,128)} %bitcast.8.packed, f32[3,96,512]{2,1,0:T(8,128)S(1)} %shard_map.189.base, ...), custom_call_target="tpu_custom_call" | custom-call | flops 5000000000 | bytes 4106240 | tf_op jit(solution)/shard_map/pallas_call | solution.py:36
  133.3 2.2 shard_map.191
  135.7 17.3 %all_to_all.61.parts = f32[16,96,128]{2,1,0:T(8,128)S(1)} all-to-all(f32[16,96,128]{2,1,0:T(8,128)S(1)} %add.27), channel_id=1, replica_groups=mesh['net'=4,'z'=4,'y'=4,'core'=2] {'z','y'}, dimensions={0} | all-to-all | bytes 1572864 | tf_op jit(solution)/shard_map/all_to_all | solution.py:380
  153.1 16.0 %all_to_all.62.current = f32[16,96,128]{2,1,0:T(8,128)S(1)} all-to-all(f32[16,96,128]{2,1,0:T(8,128)S(1)} %shard_map.192), channel_id=1, replica_groups=mesh['net'=4,'z'=4,'y'=4,'core'=2] {'z','y'}, dimensions={0} | all-to-all | bytes 1572864 | tf_op jit(solution)/shard_map/all_to_all | solution.py:380
  169.6 2.2 collective-permute-start.6
  172.7 16.5 %all_to_all.63.volts = f32[16,96,128]{2,1,0:T(8,128)S(1)} all-to-all(f32[16,96,128]{2,1,0:T(8,128)S(1)} %get-tuple-element.52), channel_id=1, replica_groups=mesh['net'=4,'z'=4,'y'=4,'core'=2] {'z','y'}, dimensions={0} | all-to-all | bytes 1572864 | tf_op jit(solution)/shard_map/all_to_all | solution.py:380
  189.2 1.5 collective-permute-start.7
  190.7 1.4 shard_map.196.before
  192.6 2.6 shard_map.197
  197.0 4.8 %all-to-all-start.8 = ((f32[128,1,1536]{2,1,0:T(1,128)}), f32[128,1,1536]{2,1,0:T(1,128)}, u32[]{:S(2)}, u32[]{:S(2)}) async-start(f32[128,1,1536]{2,1,0:T(1,128)} %bitcast.32), calls=%async_computation.8 | async-start | bytes 1572864 | tf_op jit(solution)/shard_map/all_to_all | solution.py:518
  209.5 8.5 %all-to-all-done.8 = f32[128,1,1536]{2,1,0:T(1,128)} async-done(((f32[128,1,1536]{2,1,0:T(1,128)}), f32[128,1,1536]{2,1,0:T(1,128)}, u32[]{:S(2)}, u32[]{:S(2)}) %all-to-all-start.8) | async-done | bytes 786464 | tf_op jit(solution)/shard_map/all_to_all | solution.py:518
  220.0 5.0 %shard_map.199 = (f32[3,96,512]{2,1,0:T(8,128)}, f32[3,96,512]{2,1,0:T(8,128)S(1)}, bf16[192,1536]{1,0:T(8,128)(2,1)S(1)}, f32[16,96,128]{2,1,0:T(8,128)S(1)}) custom-call(s32[4,512]{1,0:T(4,128)S(1)} %pad_add_fusion.terminal, f32[1536,128]{1,0:T(8,128)} %bitcast.10.packed, f32[3,96,512]{2,1,0:T(8,128)S(1)} %copy-done.33, f32[9,3,3,512]{3,2,1,0:T(4,128)S(1)} %copy-done.22), custom_call_target="tpu_custom_call" | custom-call | flops 5000000000 | bytes 4106240 | tf_op jit(solution)/shard_map/pallas_call | solution.py:36
  226.0 2.2 shard_map.200
  228.4 17.1 %all_to_all.64.parts = f32[16,96,128]{2,1,0:T(8,128)S(1)} all-to-all(f32[16,96,128]{2,1,0:T(8,128)S(1)} %add.28), channel_id=1, replica_groups=mesh['net'=4,'z'=4,'y'=4,'core'=2] {'z','y'}, dimensions={0} | all-to-all | bytes 1572864 | tf_op jit(solution)/shard_map/all_to_all | solution.py:380
  245.6 16.0 %all_to_all.65.current = f32[16,96,128]{2,1,0:T(8,128)S(1)} all-to-all(f32[16,96,128]{2,1,0:T(8,128)S(1)} %shard_map.201), channel_id=1, replica_groups=mesh['net'=4,'z'=4,'y'=4,'core'=2] {'z','y'}, dimensions={0} | all-to-all | bytes 1572864 | tf_op jit(solution)/shard_map/all_to_all | solution.py:380
  262.1 2.2 collective-permute-start.9
  265.9 16.5 %all_to_all.66.volts = f32[16,96,128]{2,1,0:T(8,128)S(1)} all-to-all(f32[16,96,128]{2,1,0:T(8,128)S(1)} %get-tuple-element.62), channel_id=1, replica_groups=mesh['net'=4,'z'=4,'y'=4,'core'=2] {'z','y'}, dimensions={0} | all-to-all | bytes 1572864 | tf_op jit(solution)/shard_map/all_to_all | solution.py:380
  282.3 1.5 collective-permute-start.10
  283.8 1.4 shard_map.205.before
  285.7 2.3 shard_map.206
  (131 shorter events, 36.3 us)
Async XLA Ops:
  0.6 13.7 %copy-start.4 = (f32[1,4,3,96,512]{4,3,2,1,0:T(8,128)S(1)}, f32[1,4,3,96,512]{4,3,2,1,0:T(8,128)}, u32[]{:S(2)}) copy-start(f32[1,4,3,96,512]{4,3,2,1,0:T(8,128)} %param.33) | copy-start | bytes 7077892
  2.6 21.8 %all-to-all-start = ((f32[16,96,128]{2,1,0:T(8,128)}), f32[16,96,128]{2,1,0:T(8,128)S(1)}, u32[]{:S(2)}, u32[]{:S(2)}) async-start(f32[16,96,128]{2,1,0:T(8,128)} %broadcast_in_dim.38), calls=%async_computation | async-start | bytes 1572864 | tf_op jit(solution)/shard_map/all_to_all | solution.py:380
  14.4 2.0 copy-start
  16.4 2.0 copy-start.2
  19.7 2.7 copy-start.44
  19.8 3.0 %copy-start.45 = (s32[1,512]{1,0:T(1,128)S(1)}, s32[1,512]{1,0:T(1,128)}, u32[]{:S(2)}) copy-start(s32[1,512]{1,0:T(1,128)} %param.23) | copy-start | bytes 6148
  22.5 6.2 %copy-start.16 = (f32[9,3,3,512]{3,2,1,0:T(4,128)}, f32[9,3,3,512]{3,2,1,0:T(4,128)S(1)}, u32[]{:S(2)}) copy-start(f32[9,3,3,512]{3,2,1,0:T(4,128)S(1)} %get-tuple-element.38.coef) | copy-start | bytes 497668
  24.4 4.3 %collective-permute-start = (f32[16,96,128]{2,1,0:T(8,128)S(1)}, f32[16,96,128]{2,1,0:T(8,128)}, u32[]{:S(2)}, u32[]{:S(2)}) collective-permute-start(f32[16,96,128]{2,1,0:T(8,128)S(1)} %all-to-all-done.volts), channel_id=1, source_target_pairs={{0,1},{1,0},{2,3},{3,2},{4,5},{5,4},{6,7},{7,6},{8,9},{9,8},{10,11... | collective-permute-start | bytes 2359304 | tf_op jit(solution)/shard_map/ppermute | solution.py:384
  26.7 2.0 copy-start.39
  28.1 5.9 %copy-start.47 = (s32[96]{0:T(128)S(1)}, s32[96]{0:T(128)}, u32[]{:S(2)}) copy-start(s32[96]{0:T(128)} %param.20) | copy-start | bytes 1156
  28.1 5.9 %copy-start.46 = (f32[96]{0:T(128)S(1)}, f32[96]{0:T(128)}, u32[]{:S(2)}) copy-start(f32[96]{0:T(128)} %param.21) | copy-start | bytes 1156
  28.1 6.0 %copy-start.34 = (f32[1,96,128]{2,1,0:T(8,128)S(1)}, f32[1,96,128]{2,1,0:T(8,128)}, u32[]{:S(2)}) copy-start(f32[1,96,128]{2,1,0:T(8,128)} %param.18) | copy-start | bytes 147460
  28.1 6.0 %copy-start.40 = (f32[3,1,128]{2,1,0:T(1,128)S(1)}, f32[3,1,128]{2,1,0:T(1,128)}, u32[]{:S(2)}) copy-start(f32[3,1,128]{2,1,0:T(1,128)} %source.5) | copy-start | bytes 4612
  33.5 2.8 copy-start.9
  33.5 2.8 copy-start.42
  33.5 2.8 collective-permute-start.1
  37.4 17.8 %all-to-all-start.1 = ((f32[16,96,128]{2,1,0:T(8,128)}), f32[16,96,128]{2,1,0:T(8,128)S(1)}, u32[]{:S(2)}, u32[]{:S(2)}) async-start(f32[16,96,128]{2,1,0:T(8,128)} %add.26), calls=%async_computation.1 | async-start | bytes 1572864 | tf_op jit(solution)/shard_map/all_to_all | solution.py:380
  41.4 1.6 copy-start.15
  45.3 15.2 %collective-permute-start.2 = (f32[128,2048]{1,0:T(8,128)}, f32[128,2048]{1,0:T(8,128)}, u32[]{:S(2)}, u32[]{:S(2)}) collective-permute-start(f32[128,2048]{1,0:T(8,128)} %get-tuple-element.42), channel_id=1, source_target_pairs={{0,1},{1,0},{2,3},{3,2},{4,5},{5,4},{6,7},{7,6},{8,9},{9,8},{10,11... | collective-permute-start | bytes 3145736 | tf_op jit(solution)/shard_map/ppermute | solution.py:384
  56.2 17.0 %all-to-all-start.2 = ((f32[16,96,128]{2,1,0:T(8,128)}), f32[16,96,128]{2,1,0:T(8,128)}, u32[]{:S(2)}, u32[]{:S(2)}) async-start(f32[16,96,128]{2,1,0:T(8,128)} %copy-done.8), calls=%async_computation.2 | async-start | bytes 1572864 | tf_op jit(solution)/shard_map/all_to_all | solution.py:380
  74.8 5.6 %collective-permute-start.3 = (f32[96,128]{1,0:T(8,128)S(1)}, f32[96,128]{1,0:T(8,128)S(1)}, u32[]{:S(2)}, u32[]{:S(2)}) collective-permute-start(f32[96,128]{1,0:T(8,128)S(1)} %shard_map.184), channel_id=1, source_target_pairs={{0,1},{1,0},{2,3},{3,2},{4,5},{5,4},{6,7},{7,6},{8,9},{9,8},{10,11... | collective-permute-start | bytes 147464 | tf_op jit(solution)/shard_map/ppermute | solution.py:384
  77.5 1.2 copy-start.6
  97.5 3.0 %copy-start.17 = (f32[9,3,3,512]{3,2,1,0:T(4,128)S(1)}, f32[9,3,3,512]{3,2,1,0:T(4,128)}, u32[]{:S(2)}) copy-start(f32[9,3,3,512]{3,2,1,0:T(4,128)} %copy-done.16) | copy-start | bytes 497668
  97.5 3.0 %copy-start.43 = (f32[3,96,512]{2,1,0:T(8,128)S(1)}, f32[3,96,512]{2,1,0:T(8,128)}, u32[]{:S(2)}) copy-start(f32[3,96,512]{2,1,0:T(8,128)} %copy-done.42) | copy-start | bytes 1769476
  97.5 3.0 %collective-permute-start.4 = (f32[16,96,128]{2,1,0:T(8,128)S(1)}, f32[16,96,128]{2,1,0:T(8,128)S(1)}, u32[]{:S(2)}, u32[]{:S(2)}) collective-permute-start(f32[16,96,128]{2,1,0:T(8,128)S(1)} %all_to_all.60.volts), channel_id=1, source_target_pairs={{0,1},{1,0},{2,3},{3,2},{4,5},{5,4},{6,7},{7,6},{8,9},{9,8},{10,11... | collective-permute-start | bytes 2359304 | tf_op jit(solution)/shard_map/ppermute | solution.py:384
  100.5 10.2 %copy-start.36 = (s32[1,512]{1,0:T(1,128)S(1)}, s32[1,512]{1,0:T(1,128)}, u32[]{:S(2)}) copy-start(s32[1,512]{1,0:T(1,128)} %delay.3) | copy-start | bytes 6148
  104.9 21.9 %all-to-all-start.4 = ((f32[128,1,1536]{2,1,0:T(1,128)}), f32[128,1,1536]{2,1,0:T(1,128)}, u32[]{:S(2)}, u32[]{:S(2)}) async-start(f32[128,1,1536]{2,1,0:T(1,128)} %bitcast.31), calls=%async_computation.4 | async-start | bytes 1572864 | tf_op jit(solution)/shard_map/all_to_all | solution.py:518
  110.7 2.0 copy-start.1
  112.7 2.0 copy-start.3
  115.6 4.1 %copy-start.10 = (f32[3,96,512]{2,1,0:T(8,128)S(1)}, f32[3,96,512]{2,1,0:T(8,128)}, u32[]{:S(2)}) copy-start(f32[3,96,512]{2,1,0:T(8,128)} %copy-done.9) | copy-start | bytes 1769476
  115.6 4.1 %copy-start.13 = (f32[3,96,512]{2,1,0:T(8,128)S(1)}, f32[3,96,512]{2,1,0:T(8,128)}, u32[]{:S(2)}) copy-start(f32[3,96,512]{2,1,0:T(8,128)} %copy-done.12) | copy-start | bytes 1769476
  127.7 5.6 %copy-start.41 = (f32[3,1,128]{2,1,0:T(1,128)S(1)}, f32[3,1,128]{2,1,0:T(1,128)}, u32[]{:S(2)}) copy-start(f32[3,1,128]{2,1,0:T(1,128)} %source.5) | copy-start | bytes 4612
  132.2 3.4 %copy-start.28 = (f32[3,96,512]{2,1,0:T(8,128)}, f32[3,96,512]{2,1,0:T(8,128)S(1)}, u32[]{:S(2)}) copy-start(f32[3,96,512]{2,1,0:T(8,128)S(1)} %get-tuple-element.57.a1) | copy-start | bytes 1769476
  132.2 3.4 %collective-permute-start.5 = (f32[16,96,128]{2,1,0:T(8,128)S(1)}, f32[16,96,128]{2,1,0:T(8,128)S(1)}, u32[]{:S(2)}, u32[]{:S(2)}) collective-permute-start(f32[16,96,128]{2,1,0:T(8,128)S(1)} %get-tuple-element.51), channel_id=1, source_target_pairs={{0,1},{1,0},{2,3},{3,2},{4,5},{5,4},{6,7},{7,6},{8,9},{9,8},{10,11... | collective-permute-start | bytes 2359304 | tf_op jit(solution)/shard_map/ppermute | solution.py:384
  135.7 36.1 %copy-start.7 = (bf16[256,2048]{1,0:T(8,128)(2,1)S(1)}, bf16[256,2048]{1,0:T(8,128)(2,1)}, u32[]{:S(2)}) copy-start(bf16[256,2048]{1,0:T(8,128)(2,1)} %copy-done.5) | copy-start | bytes 3145732
  169.6 3.1 %collective-permute-start.6 = (f32[96,128]{1,0:T(8,128)S(1)}, f32[96,128]{1,0:T(8,128)S(1)}, u32[]{:S(2)}, u32[]{:S(2)}) collective-permute-start(f32[96,128]{1,0:T(8,128)S(1)} %shard_map.194), channel_id=1, source_target_pairs={{0,1},{1,0},{2,3},{3,2},{4,5},{5,4},{6,7},{7,6},{8,9},{9,8},{10,11... | collective-permute-start | bytes 147464 | tf_op jit(solution)/shard_map/ppermute | solution.py:384
  189.2 3.4 %copy-start.20 = (f32[9,3,3,512]{3,2,1,0:T(4,128)S(1)}, f32[9,3,3,512]{3,2,1,0:T(4,128)}, u32[]{:S(2)}) copy-start(f32[9,3,3,512]{3,2,1,0:T(4,128)} %copy-done.16) | copy-start | bytes 497668
  189.2 3.4 %collective-permute-start.7 = (f32[16,96,128]{2,1,0:T(8,128)S(1)}, f32[16,96,128]{2,1,0:T(8,128)S(1)}, u32[]{:S(2)}, u32[]{:S(2)}) collective-permute-start(f32[16,96,128]{2,1,0:T(8,128)S(1)} %all_to_all.63.volts), channel_id=1, source_target_pairs={{0,1},{1,0},{2,3},{3,2},{4,5},{5,4},{6,7},{7,6},{8,9},{9,8},{10,11... | collective-permute-start | bytes 2359304 | tf_op jit(solution)/shard_map/ppermute | solution.py:384
  197.0 21.0 %all-to-all-start.8 = ((f32[128,1,1536]{2,1,0:T(1,128)}), f32[128,1,1536]{2,1,0:T(1,128)}, u32[]{:S(2)}, u32[]{:S(2)}) async-start(f32[128,1,1536]{2,1,0:T(1,128)} %bitcast.32), calls=%async_computation.8 | async-start | bytes 1572864 | tf_op jit(solution)/shard_map/all_to_all | solution.py:518
  201.8 1.1 copy-start.11
  202.8 1.1 copy-start.14
  204.8 1.1 copy-start.27
  207.0 1.1 copy-start.31
  218.9 1.1 copy-start.33
  225.0 3.3 %collective-permute-start.8 = (f32[16,96,128]{2,1,0:T(8,128)S(1)}, f32[16,96,128]{2,1,0:T(8,128)S(1)}, u32[]{:S(2)}, u32[]{:S(2)}) collective-permute-start(f32[16,96,128]{2,1,0:T(8,128)S(1)} %get-tuple-element.60), channel_id=1, source_target_pairs={{0,1},{1,0},{2,3},{3,2},{4,5},{5,4},{6,7},{7,6},{8,9},{9,8},{10,11... | collective-permute-start | bytes 2359304 | tf_op jit(solution)/shard_map/ppermute | solution.py:384
  262.1 3.1 %collective-permute-start.9 = (f32[96,128]{1,0:T(8,128)S(1)}, f32[96,128]{1,0:T(8,128)S(1)}, u32[]{:S(2)}, u32[]{:S(2)}) collective-permute-start(f32[96,128]{1,0:T(8,128)S(1)} %shard_map.203), channel_id=1, source_target_pairs={{0,1},{1,0},{2,3},{3,2},{4,5},{5,4},{6,7},{7,6},{8,9},{9,8},{10,11... | collective-permute-start | bytes 147464 | tf_op jit(solution)/shard_map/ppermute | solution.py:384
  282.3 3.4 %copy-start.23 = (f32[9,3,3,512]{3,2,1,0:T(4,128)S(1)}, f32[9,3,3,512]{3,2,1,0:T(4,128)}, u32[]{:S(2)}) copy-start(f32[9,3,3,512]{3,2,1,0:T(4,128)} %copy-done.16) | copy-start | bytes 497668
  282.3 3.4 %collective-permute-start.10 = (f32[16,96,128]{2,1,0:T(8,128)S(1)}, f32[16,96,128]{2,1,0:T(8,128)S(1)}, u32[]{:S(2)}, u32[]{:S(2)}) collective-permute-start(f32[16,96,128]{2,1,0:T(8,128)S(1)} %all_to_all.66.volts), channel_id=1, source_target_pairs={{0,1},{1,0},{2,3},{3,2},{4,5},{5,4},{6,7},{7,6},{8,9},{9,8},{10,11... | collective-permute-start | bytes 2359304 | tf_op jit(solution)/shard_map/ppermute | solution.py:384
  (16 other events, 14.0 us)

commit v2 on v1

--- a/solution.py
+++ b/solution.py
@@ -290,11 +290,25 @@
     return -(-CAPACITY * values // 128)
 
 
-def pack_kernel(terminal, volts, before, coef, h, term, packed, split):
+def pack_kernel(terminal, volts, before, coef, h, base, *refs):
+    *past, term, packed, known, split = refs
     gather_rest(terminal, volts, before, term, split)
     surge2 = coef[SURGE, 0, 1:2, :]
     waves = [surge2 * term[p] - h[p] for p in range(3)]
     high, low = halves(jnp.concatenate(waves, axis=0))
+    if len(past) == 1:
+        drops = [mix(coef[1], past[0]), mix(coef[0], term)]
+        gains = []
+    else:
+        drops = [mix(coef[2], past[0]), mix(coef[1], past[1]), mix(coef[0], term)]
+        gains = [mix(coef[STEPS + 1], past[2])]
+    for p in range(3):
+        value = base[p]
+        for drop in drops:
+            value = value - drop[p]
+        for gain in gains:
+            value = value + gain[p]
+        known[p] = value
     lines = packed_lines(high.shape[0])
     owners = packed.shape[0] // lines
     rows = []
@@ -305,19 +319,6 @@
     rows = jnp.concatenate(rows, axis=1)
     for k in range(lines):
         packed[pl.ds(k, owners, stride=lines), :] = rows[:, k * 128 : (k + 1) * 128]
-
-
-def known_1(base, coef, t0, t1, out):
-    a, b = mix(coef[1], t0), mix(coef[0], t1)
-    for p in range(3):
-        out[p] = base[p] - a[p] - b[p]
-
-
-def known_2(base, coef, t0, t1, t2, a1, out):
-    a, b, c = mix(coef[2], t0), mix(coef[1], t1), mix(coef[0], t2)
-    d = mix(coef[STEPS + 1], a1)
-    for p in range(3):
-        out[p] = base[p] - a[p] - b[p] - c[p] + d[p]
 
 
 def arrive_kernel(terminal, packed, base, coef, arrived, h_out, ends, out):
@@ -439,7 +440,20 @@
     def first_gather(plane):
         return call(gather_kernel, (), (table, plane), waves, [splits], 4_000_000_000)
 
-    def solve(ends_split, other, step, voltage_rows):
+    def finish_constants(states, coef, inverse):
+        later = fold(fold_later, (*small, coef), states, STEPS - 1, [])
+        mine, give = call(
+            cut_kernel,
+            (),
+            (inverse,),
+            (shape(2 * rows, CHIPS * 128, dtype=BF16), shape(rows, CHIPS * 128)),
+        )
+        other = call(
+            split_kernel, (), (swapped(give),), shape(2 * rows, CHIPS * 128, dtype=BF16)
+        )
+        return later, mine, other
+
+    def reduce(ends_split, other, step, voltage_rows):
         sent = swapped(other)
         mine = call(
             functools.partial(scatter_mine, step),
@@ -449,7 +463,10 @@
             (),
             4_000_000_000,
         )
-        plane = exchanged(call(total_kernel, (), (exchanged(mine + sent),), half))
+        return mine + sent
+
+    def solve(currents, inverse_mine, inverse_other):
+        plane = exchanged(call(total_kernel, (), (currents,), half))
         other = call(solve_kernel, (), (plane, inverse_other), block, [splits], 500_000_000)
         sent = swapped(other)
         mine = call(solve_kernel, (), (plane, inverse_mine), block, [splits], 500_000_000)
@@ -476,27 +493,25 @@
         [shape(SURGE + 1, 3, 3, slots)],
     )
     plane, base_0, coef, table = lax.optimization_barrier((plane, base_0, coef, table))
-    base = [base_0, *fold(fold_later, (*small, coef), states, STEPS - 1, [])]
-    inverse_mine, give = call(
-        cut_kernel,
-        (),
-        (conductance_inverse[0],),
-        (shape(2 * rows, CHIPS * 128, dtype=BF16), shape(rows, CHIPS * 128)),
-    )
-    inverse_other = call(
-        split_kernel, (), (swapped(give),), shape(2 * rows, CHIPS * 128, dtype=BF16)
-    )
     far = swapped(plane)
     before = first_gather(plane)
     t0, h, ends_split, other = call(
         first_kernel,
         (),
-        (table, far, before, base[0], coef),
+        (table, far, before, base_0, coef),
         (waves, waves, end_split, half),
         [splits],
         8_000_000_000,
     )
-    voltage_rows, copies = solve(ends_split, other, 0, voltage_rows)
+    currents, *inputs = lax.optimization_barrier(
+        (reduce(ends_split, other, 0, voltage_rows), states, coef, conductance_inverse[0])
+    )
+    constants = finish_constants(*inputs)
+    currents = exchanged(currents)
+    currents, constants = lax.optimization_barrier((currents, constants))
+    later, *inverses = constants
+    base = [base_0, *later]
+    voltage_rows, copies = solve(currents, *inverses)
     terms = [t0]
     arrivals = []
     lines = packed_lines(3 * scenarios)
@@ -505,11 +520,11 @@
         plane = exchanged(copies)
         far = swapped(plane)
         before = first_gather(plane)
-        term, packed = call(
+        term, packed, known = call(
             pack_kernel,
             (),
-            (table, far, before, coef, h),
-            (waves, packed_shape),
+            (table, far, before, coef, h, base[step], *terms, *arrivals),
+            (waves, packed_shape, waves),
             [splits],
             5_000_000_000,
         )
@@ -517,7 +532,6 @@
         packed = packed.reshape(devices, 1, lines * 128)
         packed = lax.all_to_all(packed, NET_LINE, 0, 0, tiled=True)
         packed = packed.reshape(devices * lines, 128)
-        known = call((known_1, known_2)[step - 1], (), (base[step], coef, *terms, *arrivals), waves)
         arrived, h, ends_split, other = call(
             arrive_kernel,
             (),
@@ -527,7 +541,8 @@
             5_000_000_000,
         )
         arrivals.append(arrived)
-        voltage_rows, copies = solve(ends_split, other, step, voltage_rows)
+        currents = exchanged(reduce(ends_split, other, step, voltage_rows))
+        voltage_rows, copies = solve(currents, *inverses)
     plane = exchanged(copies)
     far = swapped(plane)
     before = first_gather(plane)

time: 290 us -> 280 us (0.966)
  blocking collectives: 116 us -> 176 us
  waiting for transfers between devices: 40.4 us -> 5.03 us
  starting transfers between devices: 44 us -> 29 us
  local copies, waits for them, and re-layouts: 34.6 us -> 20.8 us
  Pallas kernels: 49.2 us -> 44.7 us
    all_to_all x0 -> x2, blocking collectives: none -> 41.4 us  [on_device(): packed = lax.all_to_all(packed, NET_LINE, 0, 0, tiled=True)]
    all_to_all x3 -> x2, waiting for transfers between devices: 22.4 us -> 2.08 us  [exchanged(): return lax.all_to_all(x, PLANE, 0, 0, tiled=True)]
    all_to_all x7 -> x8, blocking collectives: 116 us -> 135 us  [exchanged(): return lax.all_to_all(x, PLANE, 0, 0, tiled=True)]
    all_to_all x2 -> x0, waiting for transfers between devices: 15.2 us -> none  [on_device(): packed = lax.all_to_all(packed, NET_LINE, 0, 0, tiled=True)]
    unnamed x99 -> x83, local copies, waits for them, and re-layouts: 32.6 us -> 18.9 us
    all_to_all x2 -> x0, starting transfers between devices: 10.6 us -> none  [on_device(): packed = lax.all_to_all(packed, NET_LINE, 0, 0, tiled=True)]
    pallas_call x29 -> x27, Pallas kernels: 44.1 us -> 39.5 us  [call(): pl.pallas_call(kernel, out_shape=outs, in_specs=[SMEM] * len(scalars) + [...]
    all_to_all x3 -> x2, starting transfers between devices: 17 us -> 12.9 us  [exchanged(): return lax.all_to_all(x, PLANE, 0, 0, tiled=True)]
  transfers between devices with their start and end apart: 16 -> 13, of which waited for: 11 -> 9; matrix products, arithmetic and copies ran while one was open for 1% -> 1% of each run, Pallas kernels for 8% -> 7%
where the time goes in v2:
time: 280 us; the launch traced here: 279 us
  blocking collectives  176 us (63%)
  Pallas kernels  44.7 us (16%)
  starting transfers between devices  29 us (10%)
  local copies, waits for them, and re-layouts  20.8 us (7%)
  waiting for transfers between devices  5.03 us (2%)
    all_to_all x8, blocking collectives, exchanged(): return lax.all_to_all(x, PLANE, 0, 0, tiled=True)  135 us
    all_to_all x2, blocking collectives, on_device(): packed = lax.all_to_all(packed, NET_LINE, 0, 0, tiled=True)  41.4 us
    pallas_call x27, Pallas kernels, call(): pl.pallas_call(kernel, out_shape=outs, in_specs=[SMEM] * len(scalars) + [...  39.5 us
    unnamed x83, local copies, waits for them, and re-layouts  18.9 us
    ppermute x11, starting transfers between devices, swapped(): return lax.ppermute(x, 'core', [(0, 1), (1, 0)])  16.1 us
    all_to_all x2, starting transfers between devices, exchanged(): return lax.all_to_all(x, PLANE, 0, 0, tiled=True)  12.9 us
  transfers between devices with their start and end apart: 13, of which 9 were waited for; matrix products, arithmetic and copies ran while one was open for 1% of the time, Pallas kernels for 7%

profile of v2, /device:TPU:1, one launch (start us, length us, event | category | flops | bytes accessed | tf_op | source)
XLA Modules:
  0.0 279.0 jit_solution(2591559847161809307)
XLA Ops:
  0.6 2.0 broadcast_in_dim.38
  2.6 8.6 %all-to-all-start = ((f32[16,96,128]{2,1,0:T(8,128)}), f32[16,96,128]{2,1,0:T(8,128)S(1)}, u32[]{:S(2)}, u32[]{:S(2)}) async-start(f32[16,96,128]{2,1,0:T(8,128)} %broadcast_in_dim.38), calls=%async_computation | async-start | bytes 1572864 | tf_op jit(solution)/shard_map/all_to_all | solution.py:381
  13.3 1.0 copy_bitcast_fusion
  14.4 2.0 copy-done
  16.4 2.0 copy-done.2
  19.8 1.9 shard_map.176
  22.8 1.6 all-to-all-done.volts
  24.4 2.3 collective-permute-start
  26.7 1.4 shard_map.177.before
  28.6 3.7 %shard_map.178 = (f32[3,96,512]{2,1,0:T(8,128)S(1)}, f32[3,96,512]{2,1,0:T(8,128)S(1)}, bf16[192,1536]{1,0:T(8,128)(2,1)S(1)}, f32[16,96,128]{2,1,0:T(8,128)S(1)}) custom-call(s32[4,512]{1,0:T(4,128)S(1)} %pad_add_fusion.terminal, f32[16,96,128]{2,1,0:T(8,128)S(1)} %collective-permute-done.volts, f32[3,96,512]{2,1,0:T(8,128)S(1)} %shard_map.177.before, ...), custom_call_target="tpu_custom_call" | custom-call | flops 8000000000 | bytes 4696064 | tf_op jit(solution)/shard_map/pallas_call | solution.py:36
  33.6 2.2 shard_map.179
  35.9 1.0 add.26
  36.9 1.3 shard_map.181
  38.1 1.0 copy-done.6
  39.3 4.3 %all-to-all-start.1 = ((f32[16,96,128]{2,1,0:T(8,128)}), f32[16,96,128]{2,1,0:T(8,128)}, u32[]{:S(2)}, u32[]{:S(2)}) async-start(f32[16,96,128]{2,1,0:T(8,128)} %add.26), calls=%async_computation.1 | async-start | bytes 1572864 | tf_op jit(solution)/shard_map/all_to_all | solution.py:381
  43.6 2.0 copy-done.3
  45.6 1.7 copy-done.5
  50.3 3.3 %shard_map.180 = (f32[3,96,512]{2,1,0:T(8,128)S(1)}, f32[3,96,512]{2,1,0:T(8,128)S(1)}) custom-call(f32[1,512]{1,0:T(1,128)S(1)} %copy-done.18, s32[1,512]{1,0:T(1,128)S(1)} %copy-done.20, f32[6,512]{1,0:T(8,128)S(1)} %copy-done.13, f32[6,512]{1,0:T(8,128)S(1)} %get-tuple-element.92.pa, f32[9,3,3,512]{3,2,1,0:T(4,128)S(1)} %copy-done.10, ...), custom_call_target="tpu_custom_call" | custom-call | flops 20000000 | bytes 10811392 | tf_op jit(solution)/shard_map/pallas_call | solution.py:175
  55.2 1.5 shard_map.182.inverse
  57.2 1.2 shard_map.183
  58.4 19.1 %all_to_all.60.current = f32[16,96,128]{2,1,0:T(8,128)S(1)} all-to-all(f32[16,96,128]{2,1,0:T(8,128)S(1)} %shard_map.183), channel_id=1, replica_groups=mesh['net'=4,'z'=4,'y'=4,'core'=2] {'z','y'}, dimensions={0} | all-to-all | bytes 1572864 | tf_op jit(solution)/shard_map/all_to_all | solution.py:381
  78.1 2.2 collective-permute-start.3
  81.2 16.5 %all_to_all.61.volts = f32[16,96,128]{2,1,0:T(8,128)S(1)} all-to-all(f32[16,96,128]{2,1,0:T(8,128)S(1)} %get-tuple-element.66), channel_id=1, replica_groups=mesh['net'=4,'z'=4,'y'=4,'core'=2] {'z','y'}, dimensions={0} | all-to-all | bytes 1572864 | tf_op jit(solution)/shard_map/all_to_all | solution.py:381
  97.7 1.7 collective-permute-start.4
  99.4 1.4 shard_map.187.before
  101.3 2.8 %shard_map.188 = (f32[3,96,512]{2,1,0:T(8,128)S(1)}, f32[1536,128]{1,0:T(8,128)S(1)}, f32[3,96,512]{2,1,0:T(8,128)S(1)}) custom-call(s32[4,512]{1,0:T(4,128)S(1)} %copy-done.22, f32[16,96,128]{2,1,0:T(8,128)S(1)} %collective-permute-done.4.volts, f32[3,96,512]{2,1,0:T(8,128)S(1)} %shard_map.187.before, f32[9,3,3,512]{3,2,1,0:T(4,128)S(1)} %copy-done.11, ...), custom_call_target="tpu_custom_call" | custom-call | flops 5000000000 | bytes 5285888 | tf_op jit(solution)/shard_map/pallas_call | solution.py:36
  104.1 21.6 %all_to_all.62 = f32[128,1,1536]{2,1,0:T(1,128)S(1)} all-to-all(f32[128,1,1536]{2,1,0:T(1,128)S(1)} %bitcast.32), channel_id=1, replica_groups=mesh['net'=4,'z'=4,'y'=4,'core'=2] {'net','z','y','core'}, dimensions={0} | all-to-all | bytes 1572864 | tf_op jit(solution)/shard_map/all_to_all | solution.py:533
  125.7 3.4 %shard_map.189 = (f32[3,96,512]{2,1,0:T(8,128)S(1)}, f32[3,96,512]{2,1,0:T(8,128)S(1)}, bf16[192,1536]{1,0:T(8,128)(2,1)S(1)}, f32[16,96,128]{2,1,0:T(8,128)S(1)}) custom-call(s32[4,512]{1,0:T(4,128)S(1)} %copy-done.22, f32[1536,128]{1,0:T(8,128)S(1)} %bitcast.34, f32[3,96,512]{2,1,0:T(8,128)S(1)} %get-tuple-element.71.base, f32[9,3,3,512]{3,2,1,0:T(4,128)S(1)} %copy-done.11), custom_call_target="tpu_custom_call" | custom-call | flops 5000000000 | bytes 4106240 | tf_op jit(solution)/shard_map/pallas_call | solution.py:36
  129.1 1.1 collective-permute-start.5
  130.3 2.2 shard_map.190
  132.6 17.1 %all_to_all.63.parts = f32[16,96,128]{2,1,0:T(8,128)S(1)} all-to-all(f32[16,96,128]{2,1,0:T(8,128)S(1)} %add.27), channel_id=1, replica_groups=mesh['net'=4,'z'=4,'y'=4,'core'=2] {'z','y'}, dimensions={0} | all-to-all | bytes 1572864 | tf_op jit(solution)/shard_map/all_to_all | solution.py:381
  149.8 16.0 %all_to_all.64.current = f32[16,96,128]{2,1,0:T(8,128)S(1)} all-to-all(f32[16,96,128]{2,1,0:T(8,128)S(1)} %shard_map.191), channel_id=1, replica_groups=mesh['net'=4,'z'=4,'y'=4,'core'=2] {'z','y'}, dimensions={0} | all-to-all | bytes 1572864 | tf_op jit(solution)/shard_map/all_to_all | solution.py:381
  166.4 2.2 collective-permute-start.6
  169.5 16.5 %all_to_all.65.volts = f32[16,96,128]{2,1,0:T(8,128)S(1)} all-to-all(f32[16,96,128]{2,1,0:T(8,128)S(1)} %get-tuple-element.75), channel_id=1, replica_groups=mesh['net'=4,'z'=4,'y'=4,'core'=2] {'z','y'}, dimensions={0} | all-to-all | bytes 1572864 | tf_op jit(solution)/shard_map/all_to_all | solution.py:381
  186.0 1.5 collective-permute-start.7
  187.4 1.4 shard_map.195.before
  189.3 3.0 %shard_map.196 = (f32[3,96,512]{2,1,0:T(8,128)}, f32[1536,128]{1,0:T(8,128)S(1)}, f32[3,96,512]{2,1,0:T(8,128)S(1)}) custom-call(s32[4,512]{1,0:T(4,128)S(1)} %copy-done.22, f32[16,96,128]{2,1,0:T(8,128)S(1)} %collective-permute-done.7.volts, f32[3,96,512]{2,1,0:T(8,128)S(1)} %shard_map.195.before, f32[9,3,3,512]{3,2,1,0:T(4,128)S(1)} %copy-done.11, ...), custom_call_target="tpu_custom_call" | custom-call | flops 5000000000 | bytes 6465536 | tf_op jit(solution)/shard_map/pallas_call | solution.py:36
  192.3 19.8 %all_to_all.66 = f32[128,1,1536]{2,1,0:T(1,128)S(1)} all-to-all(f32[128,1,1536]{2,1,0:T(1,128)S(1)} %bitcast.31), channel_id=1, replica_groups=mesh['net'=4,'z'=4,'y'=4,'core'=2] {'net','z','y','core'}, dimensions={0} | all-to-all | bytes 1572864 | tf_op jit(solution)/shard_map/all_to_all | solution.py:533
  212.1 3.9 %shard_map.197 = (f32[3,96,512]{2,1,0:T(8,128)}, f32[3,96,512]{2,1,0:T(8,128)S(1)}, bf16[192,1536]{1,0:T(8,128)(2,1)S(1)}, f32[16,96,128]{2,1,0:T(8,128)S(1)}) custom-call(s32[4,512]{1,0:T(4,128)S(1)} %copy-done.22, f32[1536,128]{1,0:T(8,128)S(1)} %bitcast.33, f32[3,96,512]{2,1,0:T(8,128)S(1)} %get-tuple-element.81.base, f32[9,3,3,512]{3,2,1,0:T(4,128)S(1)} %copy-done.11), custom_call_target="tpu_custom_call" | custom-call | flops 5000000000 | bytes 4106240 | tf_op jit(solution)/shard_map/pallas_call | solution.py:36
  216.0 1.1 collective-permute-start.8
  217.1 2.2 shard_map.198
  219.4 17.1 %all_to_all.67.parts = f32[16,96,128]{2,1,0:T(8,128)S(1)} all-to-all(f32[16,96,128]{2,1,0:T(8,128)S(1)} %add.28), channel_id=1, replica_groups=mesh['net'=4,'z'=4,'y'=4,'core'=2] {'z','y'}, dimensions={0} | all-to-all | bytes 1572864 | tf_op jit(solution)/shard_map/all_to_all | solution.py:381
  236.6 16.0 %all_to_all.68.current = f32[16,96,128]{2,1,0:T(8,128)S(1)} all-to-all(f32[16,96,128]{2,1,0:T(8,128)S(1)} %shard_map.199), channel_id=1, replica_groups=mesh['net'=4,'z'=4,'y'=4,'core'=2] {'z','y'}, dimensions={0} | all-to-all | bytes 1572864 | tf_op jit(solution)/shard_map/all_to_all | solution.py:381
  253.2 2.2 collective-permute-start.9
  256.9 16.5 %all_to_all.69.volts = f32[16,96,128]{2,1,0:T(8,128)S(1)} all-to-all(f32[16,96,128]{2,1,0:T(8,128)S(1)} %get-tuple-element.86), channel_id=1, replica_groups=mesh['net'=4,'z'=4,'y'=4,'core'=2] {'z','y'}, dimensions={0} | all-to-all | bytes 1572864 | tf_op jit(solution)/shard_map/all_to_all | solution.py:381
  273.4 1.5 collective-permute-start.10
  274.8 1.4 shard_map.203.before
  276.8 2.3 shard_map.204
  (110 shorter events, 18.6 us)
Async XLA Ops:
  0.6 13.7 %copy-start.4 = (f32[1,4,3,96,512]{4,3,2,1,0:T(8,128)S(1)}, f32[1,4,3,96,512]{4,3,2,1,0:T(8,128)}, u32[]{:S(2)}) copy-start(f32[1,4,3,96,512]{4,3,2,1,0:T(8,128)} %param.33) | copy-start | bytes 7077892
  2.6 21.8 %all-to-all-start = ((f32[16,96,128]{2,1,0:T(8,128)}), f32[16,96,128]{2,1,0:T(8,128)S(1)}, u32[]{:S(2)}, u32[]{:S(2)}) async-start(f32[16,96,128]{2,1,0:T(8,128)} %broadcast_in_dim.38), calls=%async_computation | async-start | bytes 1572864 | tf_op jit(solution)/shard_map/all_to_all | solution.py:381
  11.9 9.8 %copy-start.12 = (f32[6,512]{1,0:T(8,128)}, f32[6,512]{1,0:T(8,128)S(1)}, u32[]{:S(2)}) copy-start(f32[6,512]{1,0:T(8,128)S(1)} %get-tuple-element.93.pw) | copy-start | bytes 36868
  12.6 9.1 %copy-start.17 = (f32[1,512]{1,0:T(1,128)}, f32[1,512]{1,0:T(1,128)S(1)}, u32[]{:S(2)}) copy-start(f32[1,512]{1,0:T(1,128)S(1)} %get-tuple-element.89.own) | copy-start | bytes 6148
  14.4 2.0 copy-start
  16.4 2.0 copy-start.2
  19.8 2.8 copy-start.36
  19.8 3.0 %copy-start.37 = (s32[1,512]{1,0:T(1,128)S(1)}, s32[1,512]{1,0:T(1,128)}, u32[]{:S(2)}) copy-start(s32[1,512]{1,0:T(1,128)} %param.23) | copy-start | bytes 6148
  21.7 0.8 copy-start.26
  22.5 6.0 %copy-start.9 = (f32[9,3,3,512]{3,2,1,0:T(4,128)}, f32[9,3,3,512]{3,2,1,0:T(4,128)S(1)}, u32[]{:S(2)}) copy-start(f32[9,3,3,512]{3,2,1,0:T(4,128)S(1)} %get-tuple-element.54.coef) | copy-start | bytes 497668
  22.8 10.8 %copy-start.21 = (s32[4,512]{1,0:T(4,128)}, s32[4,512]{1,0:T(4,128)S(1)}, u32[]{:S(2)}) copy-start(s32[4,512]{1,0:T(4,128)S(1)} %pad_add_fusion.terminal) | copy-start | bytes 24580
  24.4 4.2 %collective-permute-start = (f32[16,96,128]{2,1,0:T(8,128)S(1)}, f32[16,96,128]{2,1,0:T(8,128)S(1)}, u32[]{:S(2)}, u32[]{:S(2)}) collective-permute-start(f32[16,96,128]{2,1,0:T(8,128)S(1)} %all-to-all-done.volts), channel_id=1, source_target_pairs={{0,1},{1,0},{2,3},{3,2},{4,5},{5,4},{6,7},{7,6},{8,9},{9,8},{10,11... | collective-permute-start | bytes 2359304 | tf_op jit(solution)/shard_map/ppermute | solution.py:385
  26.7 1.9 copy-start.27
  28.1 5.4 %copy-start.39 = (s32[96]{0:T(128)S(1)}, s32[96]{0:T(128)}, u32[]{:S(2)}) copy-start(s32[96]{0:T(128)} %param.20) | copy-start | bytes 1156
  28.1 5.4 %copy-start.38 = (f32[96]{0:T(128)S(1)}, f32[96]{0:T(128)}, u32[]{:S(2)}) copy-start(f32[96]{0:T(128)} %param.21) | copy-start | bytes 1156
  28.1 5.5 %copy-start.14 = (f32[1,96,128]{2,1,0:T(8,128)S(1)}, f32[1,96,128]{2,1,0:T(8,128)}, u32[]{:S(2)}) copy-start(f32[1,96,128]{2,1,0:T(8,128)} %param.18) | copy-start | bytes 147460
  28.1 5.5 %copy-start.30 = (f32[3,1,128]{2,1,0:T(1,128)S(1)}, f32[3,1,128]{2,1,0:T(1,128)}, u32[]{:S(2)}) copy-start(f32[3,1,128]{2,1,0:T(1,128)} %source.5) | copy-start | bytes 4612
  32.3 0.8 copy-start.32
  33.1 2.8 copy-start.34
  33.1 2.8 %collective-permute-start.1 = (f32[16,96,128]{2,1,0:T(8,128)S(1)}, f32[16,96,128]{2,1,0:T(8,128)S(1)}, u32[]{:S(2)}, u32[]{:S(2)}) collective-permute-start(f32[16,96,128]{2,1,0:T(8,128)S(1)} %get-tuple-element.52), channel_id=1, source_target_pairs={{0,1},{1,0},{2,3},{3,2},{4,5},{5,4},{6,7},{7,6},{8,9},{9,8},{10,11... | collective-permute-start | bytes 2359304 | tf_op jit(solution)/shard_map/ppermute | solution.py:385
  33.6 2.3 copy-start.15
  33.6 3.3 %copy-start.8 = (f32[1,128,4096]{2,1,0:T(8,128)S(1)}, f32[1,128,4096]{2,1,0:T(8,128)}, u32[]{:S(2)}) copy-start(f32[1,128,4096]{2,1,0:T(8,128)} %param.17) | copy-start | bytes 6291460
  35.9 7.7 %copy-start.1 = (f32[1,6,3,96,512]{4,3,2,1,0:T(8,128)S(1)}, f32[1,6,3,96,512]{4,3,2,1,0:T(8,128)}, u32[]{:S(2)}) copy-start(f32[1,6,3,96,512]{4,3,2,1,0:T(8,128)} %param.31) | copy-start | bytes 10616836
  38.1 1.0 copy-start.6
  39.2 16.1 %collective-permute-start.2 = (f32[128,2048]{1,0:T(8,128)}, f32[128,2048]{1,0:T(8,128)}, u32[]{:S(2)}, u32[]{:S(2)}) collective-permute-start(f32[128,2048]{1,0:T(8,128)} %get-tuple-element.62), channel_id=1, source_target_pairs={{0,1},{1,0},{2,3},{3,2},{4,5},{5,4},{6,7},{7,6},{8,9},{9,8},{10,11... | collective-permute-start | bytes 3145736 | tf_op jit(solution)/shard_map/ppermute | solution.py:385
  39.3 17.9 %all-to-all-start.1 = ((f32[16,96,128]{2,1,0:T(8,128)}), f32[16,96,128]{2,1,0:T(8,128)}, u32[]{:S(2)}, u32[]{:S(2)}) async-start(f32[16,96,128]{2,1,0:T(8,128)} %add.26), calls=%async_computation.1 | async-start | bytes 1572864 | tf_op jit(solution)/shard_map/all_to_all | solution.py:381
  43.6 2.0 copy-start.3
  45.6 1.7 copy-start.5
  47.3 0.9 copy-start.10
  53.6 0.8 copy-start.24
  54.4 0.8 copy-start.28
  55.2 25.0 %copy-start.7 = (bf16[256,2048]{1,0:T(8,128)(2,1)S(1)}, bf16[256,2048]{1,0:T(8,128)(2,1)}, u32[]{:S(2)}) copy-start(bf16[256,2048]{1,0:T(8,128)(2,1)} %copy-done.6) | copy-start | bytes 3145732
  58.4 41.0 %copy-start.22 = (s32[4,512]{1,0:T(4,128)S(1)}, s32[4,512]{1,0:T(4,128)}, u32[]{:S(2)}) copy-start(s32[4,512]{1,0:T(4,128)} %copy-done.21) | copy-start | bytes 24580
  78.1 3.1 %collective-permute-start.3 = (f32[96,128]{1,0:T(8,128)S(1)}, f32[96,128]{1,0:T(8,128)S(1)}, u32[]{:S(2)}, u32[]{:S(2)}) collective-permute-start(f32[96,128]{1,0:T(8,128)S(1)} %shard_map.185), channel_id=1, source_target_pairs={{0,1},{1,0},{2,3},{3,2},{4,5},{5,4},{6,7},{7,6},{8,9},{9,8},{10,11... | collective-permute-start | bytes 147464 | tf_op jit(solution)/shard_map/ppermute | solution.py:385
  97.7 3.6 %copy-start.11 = (f32[9,3,3,512]{3,2,1,0:T(4,128)S(1)}, f32[9,3,3,512]{3,2,1,0:T(4,128)}, u32[]{:S(2)}) copy-start(f32[9,3,3,512]{3,2,1,0:T(4,128)} %copy-done.9) | copy-start | bytes 497668
  97.7 3.6 %copy-start.29 = (f32[3,96,512]{2,1,0:T(8,128)S(1)}, f32[3,96,512]{2,1,0:T(8,128)}, u32[]{:S(2)}) copy-start(f32[3,96,512]{2,1,0:T(8,128)} %copy-done.28) | copy-start | bytes 1769476
  97.7 3.6 %copy-start.33 = (f32[3,96,512]{2,1,0:T(8,128)S(1)}, f32[3,96,512]{2,1,0:T(8,128)}, u32[]{:S(2)}) copy-start(f32[3,96,512]{2,1,0:T(8,128)} %copy-done.32) | copy-start | bytes 1769476
  97.7 3.6 %copy-start.35 = (f32[3,96,512]{2,1,0:T(8,128)S(1)}, f32[3,96,512]{2,1,0:T(8,128)}, u32[]{:S(2)}) copy-start(f32[3,96,512]{2,1,0:T(8,128)} %copy-done.34) | copy-start | bytes 1769476
  97.7 3.6 %collective-permute-start.4 = (f32[16,96,128]{2,1,0:T(8,128)S(1)}, f32[16,96,128]{2,1,0:T(8,128)S(1)}, u32[]{:S(2)}, u32[]{:S(2)}) collective-permute-start(f32[16,96,128]{2,1,0:T(8,128)S(1)} %all_to_all.61.volts), channel_id=1, source_target_pairs={{0,1},{1,0},{2,3},{3,2},{4,5},{5,4},{6,7},{7,6},{8,9},{9,8},{10,11... | collective-permute-start | bytes 2359304 | tf_op jit(solution)/shard_map/ppermute | solution.py:385
  125.7 4.5 %copy-start.16 = (f32[96,128]{1,0:T(8,128)S(1)}, f32[96,128]{1,0:T(8,128)}, u32[]{:S(2)}) copy-start(f32[96,128]{1,0:T(8,128)} %copy-done.15) | copy-start | bytes 147460
  125.7 4.5 %copy-start.31 = (f32[3,1,128]{2,1,0:T(1,128)S(1)}, f32[3,1,128]{2,1,0:T(1,128)}, u32[]{:S(2)}) copy-start(f32[3,1,128]{2,1,0:T(1,128)} %source.5) | copy-start | bytes 4612
  129.1 3.4 %collective-permute-start.5 = (f32[16,96,128]{2,1,0:T(8,128)S(1)}, f32[16,96,128]{2,1,0:T(8,128)S(1)}, u32[]{:S(2)}, u32[]{:S(2)}) collective-permute-start(f32[16,96,128]{2,1,0:T(8,128)S(1)} %get-tuple-element.74), channel_id=1, source_target_pairs={{0,1},{1,0},{2,3},{3,2},{4,5},{5,4},{6,7},{7,6},{8,9},{9,8},{10,11... | collective-permute-start | bytes 2359304 | tf_op jit(solution)/shard_map/ppermute | solution.py:385
  166.4 3.1 %collective-permute-start.6 = (f32[96,128]{1,0:T(8,128)S(1)}, f32[96,128]{1,0:T(8,128)S(1)}, u32[]{:S(2)}, u32[]{:S(2)}) collective-permute-start(f32[96,128]{1,0:T(8,128)S(1)} %shard_map.193), channel_id=1, source_target_pairs={{0,1},{1,0},{2,3},{3,2},{4,5},{5,4},{6,7},{7,6},{8,9},{9,8},{10,11... | collective-permute-start | bytes 147464 | tf_op jit(solution)/shard_map/ppermute | solution.py:385
  186.0 3.4 %copy-start.25 = (f32[3,96,512]{2,1,0:T(8,128)S(1)}, f32[3,96,512]{2,1,0:T(8,128)}, u32[]{:S(2)}) copy-start(f32[3,96,512]{2,1,0:T(8,128)} %copy-done.24) | copy-start | bytes 1769476
  186.0 3.4 %collective-permute-start.7 = (f32[16,96,128]{2,1,0:T(8,128)S(1)}, f32[16,96,128]{2,1,0:T(8,128)S(1)}, u32[]{:S(2)}, u32[]{:S(2)}) collective-permute-start(f32[16,96,128]{2,1,0:T(8,128)S(1)} %all_to_all.65.volts), channel_id=1, source_target_pairs={{0,1},{1,0},{2,3},{3,2},{4,5},{5,4},{6,7},{7,6},{8,9},{9,8},{10,11... | collective-permute-start | bytes 2359304 | tf_op jit(solution)/shard_map/ppermute | solution.py:385
  216.0 3.3 %collective-permute-start.8 = (f32[16,96,128]{2,1,0:T(8,128)S(1)}, f32[16,96,128]{2,1,0:T(8,128)S(1)}, u32[]{:S(2)}, u32[]{:S(2)}) collective-permute-start(f32[16,96,128]{2,1,0:T(8,128)S(1)} %get-tuple-element.84), channel_id=1, source_target_pairs={{0,1},{1,0},{2,3},{3,2},{4,5},{5,4},{6,7},{7,6},{8,9},{9,8},{10,11... | collective-permute-start | bytes 2359304 | tf_op jit(solution)/shard_map/ppermute | solution.py:385
  253.2 3.1 %collective-permute-start.9 = (f32[96,128]{1,0:T(8,128)S(1)}, f32[96,128]{1,0:T(8,128)S(1)}, u32[]{:S(2)}, u32[]{:S(2)}) collective-permute-start(f32[96,128]{1,0:T(8,128)S(1)} %shard_map.201), channel_id=1, source_target_pairs={{0,1},{1,0},{2,3},{3,2},{4,5},{5,4},{6,7},{7,6},{8,9},{9,8},{10,11... | collective-permute-start | bytes 147464 | tf_op jit(solution)/shard_map/ppermute | solution.py:385
  273.4 3.4 %collective-permute-start.10 = (f32[16,96,128]{2,1,0:T(8,128)S(1)}, f32[16,96,128]{2,1,0:T(8,128)S(1)}, u32[]{:S(2)}, u32[]{:S(2)}) collective-permute-start(f32[16,96,128]{2,1,0:T(8,128)S(1)} %all_to_all.69.volts), channel_id=1, source_target_pairs={{0,1},{1,0},{2,3},{3,2},{4,5},{5,4},{6,7},{7,6},{8,9},{9,8},{10,11... | collective-permute-start | bytes 2359304 | tf_op jit(solution)/shard_map/ppermute | solution.py:385
  (5 other events, 3.4 us)

commit v3 on v2

--- a/solution.py
+++ b/solution.py
@@ -184,23 +184,15 @@
     )(*small, *states)
 
 
-def cut_kernel(inverse, mine, give):
+def split_kernel(inverse, far, mine, other):
     rows = inverse.shape[0]
     for k in range(CHIPS):
         lanes = slice(k * 128, (k + 1) * 128)
         start = pl.multiple_of((k * 2 + own_core()) * 128, 128)
-        high, low = halves(inverse[:, pl.ds(start, 128)])
-        mine[0:rows, lanes] = high
-        mine[rows : 2 * rows, lanes] = low
-        start = pl.multiple_of((k * 2 + 1 - own_core()) * 128, 128)
-        give[:, lanes] = inverse[:, pl.ds(start, 128)]
-
-
-def split_kernel(inverse, out):
-    rows = inverse.shape[0]
-    high, low = halves(inverse[...])
-    out[0:rows] = high
-    out[rows : 2 * rows] = low
+        for block, out in ((inverse, mine), (far, other)):
+            high, low = halves(block[:, pl.ds(start, 128)])
+            out[0:rows, lanes] = high
+            out[rows : 2 * rows, lanes] = low
 
 
 def gather_into(side, terminal, volts, split, emit):
@@ -442,15 +434,8 @@
 
     def finish_constants(states, coef, inverse):
         later = fold(fold_later, (*small, coef), states, STEPS - 1, [])
-        mine, give = call(
-            cut_kernel,
-            (),
-            (inverse,),
-            (shape(2 * rows, CHIPS * 128, dtype=BF16), shape(rows, CHIPS * 128)),
-        )
-        other = call(
-            split_kernel, (), (swapped(give),), shape(2 * rows, CHIPS * 128, dtype=BF16)
-        )
+        share = shape(2 * rows, CHIPS * 128, dtype=BF16)
+        mine, other = call(split_kernel, (), inverse, (share, share))
         return later, mine, other
 
     def reduce(ends_split, other, step, voltage_rows):
@@ -472,6 +457,7 @@
         mine = call(solve_kernel, (), (plane, inverse_mine), block, [splits], 500_000_000)
         return call(copies_kernel, (), (mine, sent), (block, half))
 
+    inverse_rows = (conductance_inverse[0], swapped(conductance_inverse[0]))
     voltage_rows = prior_voltage[0]
     plane = exchanged(jnp.broadcast_to(voltage_rows[None], half.shape))
     small = (live_float, delay_steps, pole_wave[0], pole_admit[0])
@@ -504,7 +490,7 @@
         8_000_000_000,
     )
     currents, *inputs = lax.optimization_barrier(
-        (reduce(ends_split, other, 0, voltage_rows), states, coef, conductance_inverse[0])
+        (reduce(ends_split, other, 0, voltage_rows), states, coef, inverse_rows)
     )
     constants = finish_constants(*inputs)
     currents = exchanged(currents)

time: 280 us -> 278 us (level)
  waiting for transfers between devices: 5.03 us -> 11.5 us
  local copies, waits for them, and re-layouts: 20.8 us -> 14.8 us
    unnamed x83 -> x97, local copies, waits for them, and re-layouts: 18.9 us -> 12.8 us
    all_to_all x2, waiting for transfers between devices: 2.08 us -> 7.44 us  [exchanged(): return lax.all_to_all(x, PLANE, 0, 0, tiled=True)]
    pallas_call x27 -> x26, Pallas kernels: 39.5 us -> 39.1 us  [call(): pl.pallas_call(kernel, out_shape=outs, in_specs=[SMEM] * len(scalars) + [...]
  transfers between devices with their start and end apart: 13 -> 13, of which waited for: 9 -> 9; matrix products, arithmetic and copies ran while one was open for 1% -> 1% of each run, Pallas kernels for 7% -> 9%
where the time goes in v3:
time: 278 us
  blocking collectives  176 us (63%)
  Pallas kernels  44.3 us (16%)
  starting transfers between devices  28.5 us (10%)
  local copies, waits for them, and re-layouts  14.8 us (5%)
  waiting for transfers between devices  11.5 us (4%)
    all_to_all x8, blocking collectives, exchanged(): return lax.all_to_all(x, PLANE, 0, 0, tiled=True)  134 us
    all_to_all x2, blocking collectives, on_device(): packed = lax.all_to_all(packed, NET_LINE, 0, 0, tiled=True)  41.4 us
    pallas_call x26, Pallas kernels, call(): pl.pallas_call(kernel, out_shape=outs, in_specs=[SMEM] * len(scalars) + [...  39.1 us
    ppermute x11, starting transfers between devices, swapped(): return lax.ppermute(x, 'core', [(0, 1), (1, 0)])  15.5 us
    all_to_all x2, starting transfers between devices, exchanged(): return lax.all_to_all(x, PLANE, 0, 0, tiled=True)  13 us
    unnamed x97, local copies, waits for them, and re-layouts  12.8 us
    all_to_all x2, waiting for transfers between devices, exchanged(): return lax.all_to_all(x, PLANE, 0, 0, tiled=True)  7.44 us
  transfers between devices with their start and end apart: 13, of which 9 were waited for; matrix products, arithmetic and copies ran while one was open for 1% of the time, Pallas kernels for 9%

profile of v3, /device:TPU:1, one launch (start us, length us, event | category | flops | bytes accessed | tf_op | source)
XLA Modules:
  0.0 277.5 jit_solution(15575178153995983134)
XLA Ops:
  0.7 1.9 broadcast_in_dim.38
  2.7 8.6 %all-to-all-start = ((f32[16,96,128]{2,1,0:T(8,128)}), f32[16,96,128]{2,1,0:T(8,128)S(1)}, u32[]{:S(2)}, u32[]{:S(2)}) async-start(f32[16,96,128]{2,1,0:T(8,128)} %broadcast_in_dim.38), calls=%async_computation | async-start | bytes 1572864 | tf_op jit(solution)/shard_map/all_to_all | solution.py:373
  11.5 2.0 copy-done
  13.5 2.0 copy-done.2
  15.5 1.9 shard_map.176
  18.5 5.9 %all-to-all-done.volts = f32[16,96,128]{2,1,0:T(8,128)S(1)} async-done(((f32[16,96,128]{2,1,0:T(8,128)}), f32[16,96,128]{2,1,0:T(8,128)S(1)}, u32[]{:S(2)}, u32[]{:S(2)}) %all-to-all-start) | async-done | bytes 786464 | tf_op jit(solution)/shard_map/all_to_all | solution.py:373
  24.4 2.3 collective-permute-start
  26.7 1.4 shard_map.177.before
  28.2 1.5 collective-permute-done.volts
  29.7 3.7 %shard_map.178 = (f32[3,96,512]{2,1,0:T(8,128)S(1)}, f32[3,96,512]{2,1,0:T(8,128)S(1)}, bf16[192,1536]{1,0:T(8,128)(2,1)S(1)}, f32[16,96,128]{2,1,0:T(8,128)S(1)}) custom-call(s32[4,512]{1,0:T(4,128)S(1)} %pad_add_fusion.terminal, f32[16,96,128]{2,1,0:T(8,128)S(1)} %collective-permute-done.volts, f32[3,96,512]{2,1,0:T(8,128)S(1)} %shard_map.177.before, ...), custom_call_target="tpu_custom_call" | custom-call | flops 8000000000 | bytes 4696064 | tf_op jit(solution)/shard_map/pallas_call | solution.py:36
  34.8 2.2 shard_map.179
  38.0 4.4 %all-to-all-start.1 = ((f32[16,96,128]{2,1,0:T(8,128)}), f32[16,96,128]{2,1,0:T(8,128)}, u32[]{:S(2)}, u32[]{:S(2)}) async-start(f32[16,96,128]{2,1,0:T(8,128)} %add.26), calls=%async_computation.1 | async-start | bytes 1572864 | tf_op jit(solution)/shard_map/all_to_all | solution.py:373
  42.4 1.6 copy-done.10
  44.1 2.3 shard_map.181
  46.4 1.0 copy-done.6
  47.4 1.0 copy-done.8
  48.5 1.7 copy-done.5
  50.1 3.3 %shard_map.180 = (f32[3,96,512]{2,1,0:T(8,128)S(1)}, f32[3,96,512]{2,1,0:T(8,128)S(1)}) custom-call(f32[1,512]{1,0:T(1,128)S(1)} %copy-done.20, s32[1,512]{1,0:T(1,128)S(1)} %copy-done.22, f32[6,512]{1,0:T(8,128)S(1)} %copy-done.15, f32[6,512]{1,0:T(8,128)S(1)} %get-tuple-element.94.pa, f32[9,3,3,512]{3,2,1,0:T(4,128)S(1)} %copy-done.12, ...), custom_call_target="tpu_custom_call" | custom-call | flops 20000000 | bytes 10811392 | tf_op jit(solution)/shard_map/pallas_call | solution.py:175
  55.1 1.5 all-to-all-done.1.parts
  56.7 1.3 shard_map.182
  58.0 18.6 %all_to_all.60.current = f32[16,96,128]{2,1,0:T(8,128)S(1)} all-to-all(f32[16,96,128]{2,1,0:T(8,128)S(1)} %shard_map.182), channel_id=1, replica_groups=mesh['net'=4,'z'=4,'y'=4,'core'=2] {'z','y'}, dimensions={0} | all-to-all | bytes 1572864 | tf_op jit(solution)/shard_map/all_to_all | solution.py:373
  77.1 1.6 collective-permute-start.3
  79.7 16.5 %all_to_all.61.volts = f32[16,96,128]{2,1,0:T(8,128)S(1)} all-to-all(f32[16,96,128]{2,1,0:T(8,128)S(1)} %get-tuple-element.68), channel_id=1, replica_groups=mesh['net'=4,'z'=4,'y'=4,'core'=2] {'z','y'}, dimensions={0} | all-to-all | bytes 1572864 | tf_op jit(solution)/shard_map/all_to_all | solution.py:373
  96.2 1.7 collective-permute-start.4
  97.9 1.4 shard_map.186.before
  99.8 2.8 %shard_map.187 = (f32[3,96,512]{2,1,0:T(8,128)S(1)}, f32[1536,128]{1,0:T(8,128)S(1)}, f32[3,96,512]{2,1,0:T(8,128)S(1)}) custom-call(s32[4,512]{1,0:T(4,128)S(1)} %copy-done.24, f32[16,96,128]{2,1,0:T(8,128)S(1)} %collective-permute-done.4.volts, f32[3,96,512]{2,1,0:T(8,128)S(1)} %shard_map.186.before, f32[9,3,3,512]{3,2,1,0:T(4,128)S(1)} %copy-done.13, ...), custom_call_target="tpu_custom_call" | custom-call | flops 5000000000 | bytes 5285888 | tf_op jit(solution)/shard_map/pallas_call | solution.py:36
  102.6 21.6 %all_to_all.62 = f32[128,1,1536]{2,1,0:T(1,128)S(1)} all-to-all(f32[128,1,1536]{2,1,0:T(1,128)S(1)} %bitcast.33), channel_id=1, replica_groups=mesh['net'=4,'z'=4,'y'=4,'core'=2] {'net','z','y','core'}, dimensions={0} | all-to-all | bytes 1572864 | tf_op jit(solution)/shard_map/all_to_all | solution.py:519
  124.3 3.4 %shard_map.188 = (f32[3,96,512]{2,1,0:T(8,128)S(1)}, f32[3,96,512]{2,1,0:T(8,128)S(1)}, bf16[192,1536]{1,0:T(8,128)(2,1)S(1)}, f32[16,96,128]{2,1,0:T(8,128)S(1)}) custom-call(s32[4,512]{1,0:T(4,128)S(1)} %copy-done.24, f32[1536,128]{1,0:T(8,128)S(1)} %bitcast.35, f32[3,96,512]{2,1,0:T(8,128)S(1)} %get-tuple-element.73.base, f32[9,3,3,512]{3,2,1,0:T(4,128)S(1)} %copy-done.13), custom_call_target="tpu_custom_call" | custom-call | flops 5000000000 | bytes 4106240 | tf_op jit(solution)/shard_map/pallas_call | solution.py:36
  127.6 1.2 collective-permute-start.5
  128.8 2.2 shard_map.189
  131.1 17.1 %all_to_all.63.parts = f32[16,96,128]{2,1,0:T(8,128)S(1)} all-to-all(f32[16,96,128]{2,1,0:T(8,128)S(1)} %add.27), channel_id=1, replica_groups=mesh['net'=4,'z'=4,'y'=4,'core'=2] {'z','y'}, dimensions={0} | all-to-all | bytes 1572864 | tf_op jit(solution)/shard_map/all_to_all | solution.py:373
  148.3 16.0 %all_to_all.64.current = f32[16,96,128]{2,1,0:T(8,128)S(1)} all-to-all(f32[16,96,128]{2,1,0:T(8,128)S(1)} %shard_map.190), channel_id=1, replica_groups=mesh['net'=4,'z'=4,'y'=4,'core'=2] {'z','y'}, dimensions={0} | all-to-all | bytes 1572864 | tf_op jit(solution)/shard_map/all_to_all | solution.py:373
  164.9 2.2 collective-permute-start.6
  168.0 16.5 %all_to_all.65.volts = f32[16,96,128]{2,1,0:T(8,128)S(1)} all-to-all(f32[16,96,128]{2,1,0:T(8,128)S(1)} %get-tuple-element.77), channel_id=1, replica_groups=mesh['net'=4,'z'=4,'y'=4,'core'=2] {'z','y'}, dimensions={0} | all-to-all | bytes 1572864 | tf_op jit(solution)/shard_map/all_to_all | solution.py:373
  184.5 1.5 collective-permute-start.7
  185.9 1.4 shard_map.194.before
  187.9 3.0 %shard_map.195 = (f32[3,96,512]{2,1,0:T(8,128)}, f32[1536,128]{1,0:T(8,128)S(1)}, f32[3,96,512]{2,1,0:T(8,128)S(1)}) custom-call(s32[4,512]{1,0:T(4,128)S(1)} %copy-done.24, f32[16,96,128]{2,1,0:T(8,128)S(1)} %collective-permute-done.7.volts, f32[3,96,512]{2,1,0:T(8,128)S(1)} %shard_map.194.before, f32[9,3,3,512]{3,2,1,0:T(4,128)S(1)} %copy-done.13, ...), custom_call_target="tpu_custom_call" | custom-call | flops 5000000000 | bytes 6465536 | tf_op jit(solution)/shard_map/pallas_call | solution.py:36
  190.9 19.8 %all_to_all.66 = f32[128,1,1536]{2,1,0:T(1,128)S(1)} all-to-all(f32[128,1,1536]{2,1,0:T(1,128)S(1)} %bitcast.32), channel_id=1, replica_groups=mesh['net'=4,'z'=4,'y'=4,'core'=2] {'net','z','y','core'}, dimensions={0} | all-to-all | bytes 1572864 | tf_op jit(solution)/shard_map/all_to_all | solution.py:519
  210.7 3.9 %shard_map.196 = (f32[3,96,512]{2,1,0:T(8,128)}, f32[3,96,512]{2,1,0:T(8,128)S(1)}, bf16[192,1536]{1,0:T(8,128)(2,1)S(1)}, f32[16,96,128]{2,1,0:T(8,128)S(1)}) custom-call(s32[4,512]{1,0:T(4,128)S(1)} %copy-done.24, f32[1536,128]{1,0:T(8,128)S(1)} %bitcast.34, f32[3,96,512]{2,1,0:T(8,128)S(1)} %get-tuple-element.83.base, f32[9,3,3,512]{3,2,1,0:T(4,128)S(1)} %copy-done.13), custom_call_target="tpu_custom_call" | custom-call | flops 5000000000 | bytes 4106240 | tf_op jit(solution)/shard_map/pallas_call | solution.py:36
  214.5 1.1 collective-permute-start.8
  215.6 2.2 shard_map.197
  217.9 17.1 %all_to_all.67.parts = f32[16,96,128]{2,1,0:T(8,128)S(1)} all-to-all(f32[16,96,128]{2,1,0:T(8,128)S(1)} %add.28), channel_id=1, replica_groups=mesh['net'=4,'z'=4,'y'=4,'core'=2] {'z','y'}, dimensions={0} | all-to-all | bytes 1572864 | tf_op jit(solution)/shard_map/all_to_all | solution.py:373
  235.2 16.0 %all_to_all.68.current = f32[16,96,128]{2,1,0:T(8,128)S(1)} all-to-all(f32[16,96,128]{2,1,0:T(8,128)S(1)} %shard_map.198), channel_id=1, replica_groups=mesh['net'=4,'z'=4,'y'=4,'core'=2] {'z','y'}, dimensions={0} | all-to-all | bytes 1572864 | tf_op jit(solution)/shard_map/all_to_all | solution.py:373
  251.7 2.2 collective-permute-start.9
  255.4 16.5 %all_to_all.69.volts = f32[16,96,128]{2,1,0:T(8,128)S(1)} all-to-all(f32[16,96,128]{2,1,0:T(8,128)S(1)} %get-tuple-element.88), channel_id=1, replica_groups=mesh['net'=4,'z'=4,'y'=4,'core'=2] {'z','y'}, dimensions={0} | all-to-all | bytes 1572864 | tf_op jit(solution)/shard_map/all_to_all | solution.py:373
  271.9 1.5 collective-permute-start.10
  273.4 1.4 shard_map.202.before
  275.3 2.3 shard_map.203
  (123 shorter events, 12.2 us)
Async XLA Ops:
  0.6 10.6 %copy-start.41 = (f32[1,6,512]{2,0,1:T(1,128)S(1)}, f32[1,6,512]{2,0,1:T(1,128)}, u32[]{:S(2)}) copy-start(f32[1,6,512]{2,0,1:T(1,128)} %param.29) | copy-start | bytes 36868
  0.6 10.6 %copy-start.42 = (f32[1,6,512]{2,0,1:T(1,128)S(1)}, f32[1,6,512]{2,0,1:T(1,128)}, u32[]{:S(2)}) copy-start(f32[1,6,512]{2,0,1:T(1,128)} %param.27) | copy-start | bytes 36868
  0.7 10.7 %copy-start.43 = (s32[1,512]{1,0:T(1,128)S(1)}, s32[1,512]{1,0:T(1,128)}, u32[]{:S(2)}) copy-start(s32[1,512]{1,0:T(1,128)} %param.23) | copy-start | bytes 6148
  0.7 10.7 %copy-start.44 = (s32[1,3,512]{2,0,1:T(1,128)S(1)}, s32[1,3,512]{2,0,1:T(1,128)}, u32[]{:S(2)}) copy-start(s32[1,3,512]{2,0,1:T(1,128)} %param.22) | copy-start | bytes 18436
  0.7 10.7 %copy-start.38 = (f32[1,6,3,3,512]{4,0,3,2,1:T(1,128)S(1)}, f32[1,6,3,3,512]{4,0,3,2,1:T(1,128)}, u32[]{:S(2)}) copy-start(f32[1,6,3,3,512]{4,0,3,2,1:T(1,128)} %param.30) | copy-start | bytes 331780
  0.7 10.7 %copy-start.39 = (f32[1,6,3,3,512]{4,0,3,2,1:T(1,128)S(1)}, f32[1,6,3,3,512]{4,0,3,2,1:T(1,128)}, u32[]{:S(2)}) copy-start(f32[1,6,3,3,512]{4,0,3,2,1:T(1,128)} %param.28) | copy-start | bytes 331780
  0.7 10.8 %copy-start.21 = (s32[1,512]{1,0:T(1,128)S(1)}, s32[1,512]{1,0:T(1,128)}, u32[]{:S(2)}) copy-start(s32[1,512]{1,0:T(1,128)} %delay.3) | copy-start | bytes 6148
  0.7 10.8 %copy-start.4 = (f32[1,4,3,96,512]{4,3,2,1,0:T(8,128)S(1)}, f32[1,4,3,96,512]{4,3,2,1,0:T(8,128)}, u32[]{:S(2)}) copy-start(f32[1,4,3,96,512]{4,3,2,1,0:T(8,128)} %param.33) | copy-start | bytes 7077892
  0.7 10.8 %copy-start.25 = (f32[1,512]{1,0:T(1,128)S(1)}, f32[1,512]{1,0:T(1,128)}, u32[]{:S(2)}) copy-start(f32[1,512]{1,0:T(1,128)} %surge.1) | copy-start | bytes 6148
  2.7 21.8 %all-to-all-start = ((f32[16,96,128]{2,1,0:T(8,128)}), f32[16,96,128]{2,1,0:T(8,128)S(1)}, u32[]{:S(2)}, u32[]{:S(2)}) async-start(f32[16,96,128]{2,1,0:T(8,128)} %broadcast_in_dim.38), calls=%async_computation | async-start | bytes 1572864 | tf_op jit(solution)/shard_map/all_to_all | solution.py:373
  11.3 6.1 %copy-start.14 = (f32[6,512]{1,0:T(8,128)}, f32[6,512]{1,0:T(8,128)S(1)}, u32[]{:S(2)}) copy-start(f32[6,512]{1,0:T(8,128)S(1)} %get-tuple-element.95.pw) | copy-start | bytes 36868
  11.4 6.1 %copy-start.19 = (f32[1,512]{1,0:T(1,128)}, f32[1,512]{1,0:T(1,128)S(1)}, u32[]{:S(2)}) copy-start(f32[1,512]{1,0:T(1,128)S(1)} %get-tuple-element.91.own) | copy-start | bytes 6148
  15.5 2.8 copy-start.40
  18.3 11.4 %copy-start.11 = (f32[9,3,3,512]{3,2,1,0:T(4,128)}, f32[9,3,3,512]{3,2,1,0:T(4,128)S(1)}, u32[]{:S(2)}) copy-start(f32[9,3,3,512]{3,2,1,0:T(4,128)S(1)} %get-tuple-element.55.coef) | copy-start | bytes 497668
  18.5 16.2 %copy-start.23 = (s32[4,512]{1,0:T(4,128)}, s32[4,512]{1,0:T(4,128)S(1)}, u32[]{:S(2)}) copy-start(s32[4,512]{1,0:T(4,128)S(1)} %pad_add_fusion.terminal) | copy-start | bytes 24580
  24.4 5.3 %collective-permute-start = (f32[16,96,128]{2,1,0:T(8,128)S(1)}, f32[16,96,128]{2,1,0:T(8,128)S(1)}, u32[]{:S(2)}, u32[]{:S(2)}) collective-permute-start(f32[16,96,128]{2,1,0:T(8,128)S(1)} %all-to-all-done.volts), channel_id=1, source_target_pairs={{0,1},{1,0},{2,3},{3,2},{4,5},{5,4},{6,7},{7,6},{8,9},{9,8},{10,11... | collective-permute-start | bytes 2359304 | tf_op jit(solution)/shard_map/ppermute | solution.py:377
  26.7 11.3 %collective-permute-start.2 = (f32[128,4096]{1,0:T(8,128)}, f32[128,4096]{1,0:T(8,128)}, u32[]{:S(2)}, u32[]{:S(2)}) collective-permute-start(f32[128,4096]{1,0:T(8,128)} %bitcast.30), channel_id=1, source_target_pairs={{0,1},{1,0},{2,3},{3,2},{4,5},{5,4},{6,7},{7,6},{8,9},{9,8},{10,11... | collective-permute-start | bytes 6291464 | tf_op jit(solution)/shard_map/ppermute | solution.py:377
  26.7 3.0 %copy-start.29 = (f32[3,96,512]{2,1,0:T(8,128)S(1)}, f32[3,96,512]{2,1,0:T(8,128)}, u32[]{:S(2)}) copy-start(f32[3,96,512]{2,1,0:T(8,128)} %copy-done.28) | copy-start | bytes 1769476
  28.1 6.5 %copy-start.46 = (s32[96]{0:T(128)S(1)}, s32[96]{0:T(128)}, u32[]{:S(2)}) copy-start(s32[96]{0:T(128)} %param.20) | copy-start | bytes 1156
  28.2 6.5 %copy-start.45 = (f32[96]{0:T(128)S(1)}, f32[96]{0:T(128)}, u32[]{:S(2)}) copy-start(f32[96]{0:T(128)} %param.21) | copy-start | bytes 1156
  28.2 6.6 %copy-start.16 = (f32[1,96,128]{2,1,0:T(8,128)S(1)}, f32[1,96,128]{2,1,0:T(8,128)}, u32[]{:S(2)}) copy-start(f32[1,96,128]{2,1,0:T(8,128)} %param.18) | copy-start | bytes 147460
  28.2 6.6 %copy-start.32 = (f32[3,1,128]{2,1,0:T(1,128)S(1)}, f32[3,1,128]{2,1,0:T(1,128)}, u32[]{:S(2)}) copy-start(f32[3,1,128]{2,1,0:T(1,128)} %source.5) | copy-start | bytes 4612
  34.2 2.8 collective-permute-start.1
  37.0 11.4 %copy-start.3 = (f32[1,6,3,96,512]{4,3,2,1,0:T(8,128)S(1)}, f32[1,6,3,96,512]{4,3,2,1,0:T(8,128)}, u32[]{:S(2)}) copy-start(f32[1,6,3,96,512]{4,3,2,1,0:T(8,128)} %param.32) | copy-start | bytes 10616836
  38.0 18.6 %all-to-all-start.1 = ((f32[16,96,128]{2,1,0:T(8,128)}), f32[16,96,128]{2,1,0:T(8,128)}, u32[]{:S(2)}, u32[]{:S(2)}) async-start(f32[16,96,128]{2,1,0:T(8,128)} %add.26), calls=%async_computation.1 | async-start | bytes 1572864 | tf_op jit(solution)/shard_map/all_to_all | solution.py:373
  44.0 4.4 %copy-start.1 = (f32[1,6,3,96,512]{4,3,2,1,0:T(8,128)S(1)}, f32[1,6,3,96,512]{4,3,2,1,0:T(8,128)}, u32[]{:S(2)}) copy-start(f32[1,6,3,96,512]{4,3,2,1,0:T(8,128)} %param.31) | copy-start | bytes 10616836
  44.0 4.4 %copy-start.12 = (f32[9,3,3,512]{3,2,1,0:T(4,128)S(1)}, f32[9,3,3,512]{3,2,1,0:T(4,128)}, u32[]{:S(2)}) copy-start(f32[9,3,3,512]{3,2,1,0:T(4,128)} %copy-done.11) | copy-start | bytes 497668
  44.0 4.4 %copy-start.15 = (f32[6,512]{1,0:T(8,128)S(1)}, f32[6,512]{1,0:T(8,128)}, u32[]{:S(2)}) copy-start(f32[6,512]{1,0:T(8,128)} %copy-done.14) | copy-start | bytes 36868
  44.0 4.4 %copy-start.20 = (f32[1,512]{1,0:T(1,128)S(1)}, f32[1,512]{1,0:T(1,128)}, u32[]{:S(2)}) copy-start(f32[1,512]{1,0:T(1,128)} %copy-done.19) | copy-start | bytes 6148
  44.0 4.4 %copy-start.22 = (s32[1,512]{1,0:T(1,128)S(1)}, s32[1,512]{1,0:T(1,128)}, u32[]{:S(2)}) copy-start(s32[1,512]{1,0:T(1,128)} %delay.3) | copy-start | bytes 6148
  55.1 21.5 %copy-start.9 = (bf16[256,2048]{1,0:T(8,128)(2,1)S(1)}, bf16[256,2048]{1,0:T(8,128)(2,1)}, u32[]{:S(2)}) copy-start(bf16[256,2048]{1,0:T(8,128)(2,1)} %copy-done.8) | copy-start | bytes 3145732
  56.7 22.1 %copy-start.7 = (bf16[256,2048]{1,0:T(8,128)(2,1)S(1)}, bf16[256,2048]{1,0:T(8,128)(2,1)}, u32[]{:S(2)}) copy-start(bf16[256,2048]{1,0:T(8,128)(2,1)} %copy-done.6) | copy-start | bytes 3145732
  76.6 21.3 %copy-start.24 = (s32[4,512]{1,0:T(4,128)S(1)}, s32[4,512]{1,0:T(4,128)}, u32[]{:S(2)}) copy-start(s32[4,512]{1,0:T(4,128)} %copy-done.23) | copy-start | bytes 24580
  77.1 2.5 collective-permute-start.3
  96.2 3.6 %copy-start.13 = (f32[9,3,3,512]{3,2,1,0:T(4,128)S(1)}, f32[9,3,3,512]{3,2,1,0:T(4,128)}, u32[]{:S(2)}) copy-start(f32[9,3,3,512]{3,2,1,0:T(4,128)} %copy-done.11) | copy-start | bytes 497668
  96.2 3.6 %copy-start.31 = (f32[3,96,512]{2,1,0:T(8,128)S(1)}, f32[3,96,512]{2,1,0:T(8,128)}, u32[]{:S(2)}) copy-start(f32[3,96,512]{2,1,0:T(8,128)} %copy-done.30) | copy-start | bytes 1769476
  96.2 3.6 %copy-start.35 = (f32[3,96,512]{2,1,0:T(8,128)S(1)}, f32[3,96,512]{2,1,0:T(8,128)}, u32[]{:S(2)}) copy-start(f32[3,96,512]{2,1,0:T(8,128)} %copy-done.34) | copy-start | bytes 1769476
  96.2 3.6 %copy-start.37 = (f32[3,96,512]{2,1,0:T(8,128)S(1)}, f32[3,96,512]{2,1,0:T(8,128)}, u32[]{:S(2)}) copy-start(f32[3,96,512]{2,1,0:T(8,128)} %copy-done.36) | copy-start | bytes 1769476
  96.2 3.6 %collective-permute-start.4 = (f32[16,96,128]{2,1,0:T(8,128)S(1)}, f32[16,96,128]{2,1,0:T(8,128)S(1)}, u32[]{:S(2)}, u32[]{:S(2)}) collective-permute-start(f32[16,96,128]{2,1,0:T(8,128)S(1)} %all_to_all.61.volts), channel_id=1, source_target_pairs={{0,1},{1,0},{2,3},{3,2},{4,5},{5,4},{6,7},{7,6},{8,9},{9,8},{10,11... | collective-permute-start | bytes 2359304 | tf_op jit(solution)/shard_map/ppermute | solution.py:377
  124.2 4.5 %copy-start.18 = (f32[96,128]{1,0:T(8,128)S(1)}, f32[96,128]{1,0:T(8,128)}, u32[]{:S(2)}) copy-start(f32[96,128]{1,0:T(8,128)} %copy-done.17) | copy-start | bytes 147460
  124.3 4.5 %copy-start.33 = (f32[3,1,128]{2,1,0:T(1,128)S(1)}, f32[3,1,128]{2,1,0:T(1,128)}, u32[]{:S(2)}) copy-start(f32[3,1,128]{2,1,0:T(1,128)} %source.5) | copy-start | bytes 4612
  127.6 3.4 %collective-permute-start.5 = (f32[16,96,128]{2,1,0:T(8,128)S(1)}, f32[16,96,128]{2,1,0:T(8,128)S(1)}, u32[]{:S(2)}, u32[]{:S(2)}) collective-permute-start(f32[16,96,128]{2,1,0:T(8,128)S(1)} %get-tuple-element.76), channel_id=1, source_target_pairs={{0,1},{1,0},{2,3},{3,2},{4,5},{5,4},{6,7},{7,6},{8,9},{9,8},{10,11... | collective-permute-start | bytes 2359304 | tf_op jit(solution)/shard_map/ppermute | solution.py:377
  164.9 3.1 %collective-permute-start.6 = (f32[96,128]{1,0:T(8,128)S(1)}, f32[96,128]{1,0:T(8,128)S(1)}, u32[]{:S(2)}, u32[]{:S(2)}) collective-permute-start(f32[96,128]{1,0:T(8,128)S(1)} %shard_map.192), channel_id=1, source_target_pairs={{0,1},{1,0},{2,3},{3,2},{4,5},{5,4},{6,7},{7,6},{8,9},{9,8},{10,11... | collective-permute-start | bytes 147464 | tf_op jit(solution)/shard_map/ppermute | solution.py:377
  184.5 3.4 %copy-start.27 = (f32[3,96,512]{2,1,0:T(8,128)S(1)}, f32[3,96,512]{2,1,0:T(8,128)}, u32[]{:S(2)}) copy-start(f32[3,96,512]{2,1,0:T(8,128)} %copy-done.26) | copy-start | bytes 1769476
  184.5 3.4 %collective-permute-start.7 = (f32[16,96,128]{2,1,0:T(8,128)S(1)}, f32[16,96,128]{2,1,0:T(8,128)S(1)}, u32[]{:S(2)}, u32[]{:S(2)}) collective-permute-start(f32[16,96,128]{2,1,0:T(8,128)S(1)} %all_to_all.65.volts), channel_id=1, source_target_pairs={{0,1},{1,0},{2,3},{3,2},{4,5},{5,4},{6,7},{7,6},{8,9},{9,8},{10,11... | collective-permute-start | bytes 2359304 | tf_op jit(solution)/shard_map/ppermute | solution.py:377
  214.5 3.3 %collective-permute-start.8 = (f32[16,96,128]{2,1,0:T(8,128)S(1)}, f32[16,96,128]{2,1,0:T(8,128)S(1)}, u32[]{:S(2)}, u32[]{:S(2)}) collective-permute-start(f32[16,96,128]{2,1,0:T(8,128)S(1)} %get-tuple-element.86), channel_id=1, source_target_pairs={{0,1},{1,0},{2,3},{3,2},{4,5},{5,4},{6,7},{7,6},{8,9},{9,8},{10,11... | collective-permute-start | bytes 2359304 | tf_op jit(solution)/shard_map/ppermute | solution.py:377
  251.7 3.1 %collective-permute-start.9 = (f32[96,128]{1,0:T(8,128)S(1)}, f32[96,128]{1,0:T(8,128)S(1)}, u32[]{:S(2)}, u32[]{:S(2)}) collective-permute-start(f32[96,128]{1,0:T(8,128)S(1)} %shard_map.200), channel_id=1, source_target_pairs={{0,1},{1,0},{2,3},{3,2},{4,5},{5,4},{6,7},{7,6},{8,9},{9,8},{10,11... | collective-permute-start | bytes 147464 | tf_op jit(solution)/shard_map/ppermute | solution.py:377
  271.9 3.4 %collective-permute-start.10 = (f32[16,96,128]{2,1,0:T(8,128)S(1)}, f32[16,96,128]{2,1,0:T(8,128)S(1)}, u32[]{:S(2)}, u32[]{:S(2)}) collective-permute-start(f32[16,96,128]{2,1,0:T(8,128)S(1)} %all_to_all.69.volts), channel_id=1, source_target_pairs={{0,1},{1,0},{2,3},{3,2},{4,5},{5,4},{6,7},{7,6},{8,9},{9,8},{10,11... | collective-permute-start | bytes 2359304 | tf_op jit(solution)/shard_map/ppermute | solution.py:377
  (12 other events, 17.7 us)
